TPU v7x, 512 devices: a whole 4x4x16 slice. The times are simulated.
512 devices in a mesh: gx: 16 (over z), gy: 32 (over x, y, core).
Axes of the slice: x: 4, y: 4, z: 16, core: 2. Of those that a mesh axis runs over, the one named last changes fastest.
Arguments:
- state: bfloat16 [2, 16, 512, 4096], P(None, None, 'gx', 'gy'), may hold values from -6 to 6
- potential: float32 [512, 4096], P('gx', 'gy'), may hold values from -1 to 1
- bonds: int32 [2, 512, 4096], P(None, 'gx', 'gy'), may hold values 0 or 1
- coeffs: float32 [4], replicated, may hold values from 0.3 to 0.9
- boundary: int32 [1], replicated, may hold values from 1024 to 3071
- counting: float32 [1], replicated, may hold values from 0.5 to 2.5
Outputs:
- evolved: bfloat16 [2, 16, 512, 4096], P(None, None, 'gx', 'gy')
- intersection: float32 [2, 16, 16], replicated
All inputs are finite; a program needn't handle non-finite values. No bound on the sum of `bonds` on one device may be relied on, other than what follows from the above.
Results may differ from a plain program's by a relative error of at most 0.0013.
Values sent between devices are 32-bit elements; how exact they have to be, the bound alone decides.
No kernel may reach another device: no remote copies, remote signals or barrier semaphores. Data moves between devices by JAX's collectives and lax.ppermute only.
A program may use at most 64 MiB of HBM per device.

v0:
```python
import jax
import jax.numpy as jnp
from jax import lax
from jax.sharding import PartitionSpec as P

STEPS = 3


energy_scale = 5.0


def passed_along(array, axis, by):
    peers = lax.axis_size(axis)
    pairs = [(i, i + by) for i in range(peers) if 0 <= i + by < peers]
    return lax.ppermute(array, axis, pairs)


def on_device(state, potential, bonds, coeffs, boundary, counting):
    mask_row = bonds[0].astype(jnp.float32)
    mask_col = bonds[1].astype(jnp.float32)
    rows_here = state.shape[2]
    cols_here = state.shape[3]

    def hamilton(wave):
        moved_row = mask_row * wave
        moved_col = mask_col * wave
        below_rim = passed_along(wave[:, :, :1, :], "gx", -1)
        above_rim = passed_along(moved_row[:, :, -1:, :], "gx", 1)
        right_rim = passed_along(wave[:, :, :, :1], "gy", -1)
        left_rim = passed_along(moved_col[:, :, :, -1:], "gy", 1)
        below = jnp.concatenate([wave[:, :, 1:, :], below_rim], axis=2)
        above = jnp.concatenate([above_rim, moved_row[:, :, :-1, :]], axis=2)
        right_side = jnp.concatenate([wave[:, :, :, 1:], right_rim], axis=3)
        left_side = jnp.concatenate([left_rim, moved_col[:, :, :, :-1]], axis=3)
        hopping = mask_row * below + above + mask_col * right_side + left_side
        return (potential * wave - hopping) / energy_scale

    current = state.astype(jnp.float32)
    for repeat in range(STEPS):
        term_zero = current
        term_one = hamilton(term_zero)
        term_two = 2.0 * hamilton(term_one) - term_zero
        term_three = 2.0 * hamilton(term_two) - term_one
        real_part = (
            coeffs[0] * term_zero[0]
            + coeffs[1] * term_one[1]
            - coeffs[2] * term_two[0]
            - coeffs[3] * term_three[1]
        )
        imag_part = (
            coeffs[0] * term_zero[1]
            - coeffs[1] * term_one[0]
            - coeffs[2] * term_two[1]
            + coeffs[3] * term_three[0]
        )
        current = jnp.stack([real_part, imag_part])
    evolved = current.astype(jnp.bfloat16)
    norbit = evolved.shape[1]
    flat = evolved.reshape(2, norbit, rows_here * cols_here)
    col_start = lax.axis_index("gy") * cols_here
    local_cols = jnp.arange(cols_here, dtype=jnp.int32) + col_start
    inside_cols = (local_cols >= boundary[0]).astype(jnp.bfloat16)
    inside = jnp.tile(inside_cols, rows_here)
    real_amp, imag_amp = (flat[0], flat[1])
    real_right, imag_right = (real_amp * inside, imag_amp * inside)
    total_re = jnp.dot(real_amp, real_amp.T, preferred_element_type=jnp.float32) + jnp.dot(
        imag_amp, imag_amp.T, preferred_element_type=jnp.float32
    )
    total_im = jnp.dot(real_amp, imag_amp.T, preferred_element_type=jnp.float32) - jnp.dot(
        imag_amp, real_amp.T, preferred_element_type=jnp.float32
    )
    right_re = jnp.dot(real_amp, real_right.T, preferred_element_type=jnp.float32) + jnp.dot(
        imag_amp, imag_right.T, preferred_element_type=jnp.float32
    )
    right_im = jnp.dot(real_amp, imag_right.T, preferred_element_type=jnp.float32) - jnp.dot(
        imag_amp, real_right.T, preferred_element_type=jnp.float32
    )
    partial_sums = jnp.stack([total_re, total_im, right_re, right_im])
    summed = lax.psum(partial_sums, ("gx", "gy"))
    count = float(rows_here * lax.axis_size("gx") * cols_here * lax.axis_size("gy"))
    cosine = jnp.cos(counting[0]) - 1.0
    sine = jnp.sin(counting[0])
    over_re = (summed[0] + cosine * summed[2] - sine * summed[3]) / count
    over_im = (summed[1] + cosine * summed[3] + sine * summed[2]) / count
    return (evolved, jnp.stack([over_re, over_im]))


def solution(mesh):
    return jax.shard_map(
        on_device,
        mesh=mesh,
        in_specs=(P(None, None, "gx", "gy"), P("gx", "gy"), P(None, "gx", "gy"), P(), P(), P()),
        out_specs=(P(None, None, "gx", "gy"), P()),
        check_vma=False,
    )
```

profile of v0, /device:TPU:1, one launch (start us, length us, event | category | flops | bytes accessed | tf_op | source)
XLA Modules:
  0.0 317.4 jit_solution(245137370929176669)
XLA Ops:
  2.7 4.6 %collective-permute-start.3 = (f32[2,16,32,1]{3,2,1,0:T(8,128)S(1)}, f32[2,16,32,1]{3,2,1,0:T(8,128)S(1)}, u32[]{:S(2)}, u32[]{:S(2)}) collective-permute-start(f32[2,16,32,1]{3,2,1,0:T(8,128)S(1)} %slice.447), channel_id=1, source_target_pairs={{0,1},{1,2},{2,3},{3,4},{4,5},{5,6},{6,7},{7,8},{8,9},{9,10},{10,1... | collective-permute-start | bytes 12296 | tf_op jit(solution)/shard_map/ppermute | solution.py:15
  15.8 5.6 %collective-permute-done.2 = f32[2,16,32,1]{3,2,1,0:T(8,128)S(1)} collective-permute-done((f32[2,16,32,1]{3,2,1,0:T(8,128)S(1)}, f32[2,16,32,1]{3,2,1,0:T(8,128)S(1)}, u32[]{:S(2)}, u32[]{:S(2)}) %collective-permute-start.2) | collective-permute-done | bytes 4128 | tf_op jit(solution)/shard_map/ppermute | solution.py:15
  25.4 4.2 %collective-permute-start.5 = (f32[2,16,1,128]{3,2,1,0:T(1,128)S(1)}, f32[2,16,1,128]{3,2,1,0:T(1,128)S(1)}, u32[]{:S(2)}, u32[]{:S(2)}) collective-permute-start(f32[2,16,1,128]{3,2,1,0:T(1,128)S(1)} %slice.452), channel_id=1, source_target_pairs={{0,32},{32,64},{64,96},{96,128},{128,160},{160,192},{192,224},{224... | collective-permute-start | bytes 49160 | tf_op jit(solution)/shard_map/ppermute | solution.py:15
  29.8 4.0 %collective-permute-start.7 = (f32[2,16,32,1]{3,2,1,0:T(8,128)S(1)}, f32[2,16,32,1]{3,2,1,0:T(8,128)S(1)}, u32[]{:S(2)}, u32[]{:S(2)}) collective-permute-start(f32[2,16,32,1]{3,2,1,0:T(8,128)S(1)} %slice.456), channel_id=1, source_target_pairs={{0,1},{1,2},{2,3},{3,4},{4,5},{5,6},{6,7},{7,8},{8,9},{9,10},{10,1... | collective-permute-start | bytes 12296 | tf_op jit(solution)/shard_map/ppermute | solution.py:15
  34.1 5.8 %collective-permute-done.7 = f32[2,16,32,1]{3,2,1,0:T(8,128)S(1)} collective-permute-done((f32[2,16,32,1]{3,2,1,0:T(8,128)S(1)}, f32[2,16,32,1]{3,2,1,0:T(8,128)S(1)}, u32[]{:S(2)}, u32[]{:S(2)}) %collective-permute-start.7) | collective-permute-done | bytes 4128 | tf_op jit(solution)/shard_map/ppermute | solution.py:15
  40.8 4.4 %collective-permute-start.11 = (f32[2,16,32,1]{3,2,1,0:T(8,128)S(1)}, f32[2,16,32,1]{3,2,1,0:T(8,128)S(1)}, u32[]{:S(2)}, u32[]{:S(2)}) collective-permute-start(f32[2,16,32,1]{3,2,1,0:T(8,128)S(1)} %slice.465), channel_id=1, source_target_pairs={{0,1},{1,2},{2,3},{3,4},{4,5},{5,6},{6,7},{7,8},{8,9},{9,10},{10,1... | collective-permute-start | bytes 12296 | tf_op jit(solution)/shard_map/ppermute | solution.py:15
  53.0 6.3 %collective-permute-done.10 = f32[2,16,32,1]{3,2,1,0:T(8,128)S(1)} collective-permute-done((f32[2,16,32,1]{3,2,1,0:T(8,128)S(1)}, f32[2,16,32,1]{3,2,1,0:T(8,128)S(1)}, u32[]{:S(2)}, u32[]{:S(2)}) %collective-permute-start.10) | collective-permute-done | bytes 4128 | tf_op jit(solution)/shard_map/ppermute | solution.py:15
  66.3 3.6 %collective-permute-start.15 = (f32[2,16,32,1]{3,2,1,0:T(8,128)S(1)}, f32[2,16,32,1]{3,2,1,0:T(8,128)S(1)}, u32[]{:S(2)}, u32[]{:S(2)}) collective-permute-start(f32[2,16,32,1]{3,2,1,0:T(8,128)S(1)} %slice.482), channel_id=1, source_target_pairs={{0,1},{1,2},{2,3},{3,4},{4,5},{5,6},{6,7},{7,8},{8,9},{9,10},{10,1... | collective-permute-start | bytes 12296 | tf_op jit(solution)/shard_map/ppermute | solution.py:15
  69.9 5.3 %collective-permute-start.13 = (f32[2,16,1,128]{3,2,1,0:T(1,128)S(1)}, f32[2,16,1,128]{3,2,1,0:T(1,128)S(1)}, u32[]{:S(2)}, u32[]{:S(2)}) collective-permute-start(f32[2,16,1,128]{3,2,1,0:T(1,128)S(1)} %slice.476), channel_id=1, source_target_pairs={{0,32},{32,64},{64,96},{96,128},{128,160},{160,192},{192,224},{224... | collective-permute-start | bytes 49160 | tf_op jit(solution)/shard_map/ppermute | solution.py:15
  78.2 5.9 %collective-permute-start.17 = (f32[2,16,1,128]{3,2,1,0:T(1,128)S(1)}, f32[2,16,1,128]{3,2,1,0:T(1,128)S(1)}, u32[]{:S(2)}, u32[]{:S(2)}) collective-permute-start(f32[2,16,1,128]{3,2,1,0:T(1,128)S(1)} %slice.487), channel_id=1, source_target_pairs={{0,32},{32,64},{64,96},{96,128},{128,160},{160,192},{192,224},{224... | collective-permute-start | bytes 49160 | tf_op jit(solution)/shard_map/ppermute | solution.py:15
  86.1 4.7 %collective-permute-start.19 = (f32[2,16,32,1]{3,2,1,0:T(8,128)S(1)}, f32[2,16,32,1]{3,2,1,0:T(8,128)S(1)}, u32[]{:S(2)}, u32[]{:S(2)}) collective-permute-start(f32[2,16,32,1]{3,2,1,0:T(8,128)S(1)} %slice.491), channel_id=1, source_target_pairs={{0,1},{1,2},{2,3},{3,4},{4,5},{5,6},{6,7},{7,8},{8,9},{9,10},{10,1... | collective-permute-start | bytes 12296 | tf_op jit(solution)/shard_map/ppermute | solution.py:15
  91.1 4.5 %collective-permute-done.18 = f32[2,16,32,1]{3,2,1,0:T(8,128)S(1)} collective-permute-done((f32[2,16,32,1]{3,2,1,0:T(8,128)S(1)}, f32[2,16,32,1]{3,2,1,0:T(8,128)S(1)}, u32[]{:S(2)}, u32[]{:S(2)}) %collective-permute-start.18) | collective-permute-done | bytes 4128 | tf_op jit(solution)/shard_map/ppermute | solution.py:15
  97.6 4.9 %collective-permute-start.21 = (f32[2,16,1,128]{3,2,1,0:T(1,128)S(1)}, f32[2,16,1,128]{3,2,1,0:T(1,128)S(1)}, u32[]{:S(2)}, u32[]{:S(2)}) collective-permute-start(f32[2,16,1,128]{3,2,1,0:T(1,128)S(1)} %slice.496), channel_id=1, source_target_pairs={{0,32},{32,64},{64,96},{96,128},{128,160},{160,192},{192,224},{224... | collective-permute-start | bytes 49160 | tf_op jit(solution)/shard_map/ppermute | solution.py:15
  103.9 4.7 %collective-permute-start.23 = (f32[2,16,32,1]{3,2,1,0:T(8,128)S(1)}, f32[2,16,32,1]{3,2,1,0:T(8,128)S(1)}, u32[]{:S(2)}, u32[]{:S(2)}) collective-permute-start(f32[2,16,32,1]{3,2,1,0:T(8,128)S(1)} %slice.500), channel_id=1, source_target_pairs={{0,1},{1,2},{2,3},{3,4},{4,5},{5,6},{6,7},{7,8},{8,9},{9,10},{10,1... | collective-permute-start | bytes 12296 | tf_op jit(solution)/shard_map/ppermute | solution.py:15
  110.8 3.9 %collective-permute-done.23 = f32[2,16,32,1]{3,2,1,0:T(8,128)S(1)} collective-permute-done((f32[2,16,32,1]{3,2,1,0:T(8,128)S(1)}, f32[2,16,32,1]{3,2,1,0:T(8,128)S(1)}, u32[]{:S(2)}, u32[]{:S(2)}) %collective-permute-start.23) | collective-permute-done | bytes 4128 | tf_op jit(solution)/shard_map/ppermute | solution.py:15
  114.7 4.4 %collective-permute-done.22 = f32[2,16,32,1]{3,2,1,0:T(8,128)S(1)} collective-permute-done((f32[2,16,32,1]{3,2,1,0:T(8,128)S(1)}, f32[2,16,32,1]{3,2,1,0:T(8,128)S(1)}, u32[]{:S(2)}, u32[]{:S(2)}) %collective-permute-start.22) | collective-permute-done | bytes 4128 | tf_op jit(solution)/shard_map/ppermute | solution.py:15
  129.7 4.9 %collective-permute-start.25 = (f32[2,16,1,128]{3,2,1,0:T(1,128)S(1)}, f32[2,16,1,128]{3,2,1,0:T(1,128)S(1)}, u32[]{:S(2)}, u32[]{:S(2)}) collective-permute-start(f32[2,16,1,128]{3,2,1,0:T(1,128)S(1)} %slice.510), channel_id=1, source_target_pairs={{0,32},{32,64},{64,96},{96,128},{128,160},{160,192},{192,224},{224... | collective-permute-start | bytes 49160 | tf_op jit(solution)/shard_map/ppermute | solution.py:15
  137.9 5.5 %collective-permute-start.29 = (f32[2,16,1,128]{3,2,1,0:T(1,128)S(1)}, f32[2,16,1,128]{3,2,1,0:T(1,128)S(1)}, u32[]{:S(2)}, u32[]{:S(2)}) collective-permute-start(f32[2,16,1,128]{3,2,1,0:T(1,128)S(1)} %slice.521), channel_id=1, source_target_pairs={{0,32},{32,64},{64,96},{96,128},{128,160},{160,192},{192,224},{224... | collective-permute-start | bytes 49160 | tf_op jit(solution)/shard_map/ppermute | solution.py:15
  145.6 4.7 %collective-permute-start.31 = (f32[2,16,32,1]{3,2,1,0:T(8,128)S(1)}, f32[2,16,32,1]{3,2,1,0:T(8,128)}, u32[]{:S(2)}, u32[]{:S(2)}) collective-permute-start(f32[2,16,32,1]{3,2,1,0:T(8,128)S(1)} %slice.525), channel_id=1, source_target_pairs={{0,1},{1,2},{2,3},{3,4},{4,5},{5,6},{6,7},{7,8},{8,9},{9,10},{10,1... | collective-permute-start | bytes 12296 | tf_op jit(solution)/shard_map/ppermute | solution.py:15
  151.1 3.9 %collective-permute-done.30 = f32[2,16,32,1]{3,2,1,0:T(8,128)} collective-permute-done((f32[2,16,32,1]{3,2,1,0:T(8,128)S(1)}, f32[2,16,32,1]{3,2,1,0:T(8,128)}, u32[]{:S(2)}, u32[]{:S(2)}) %collective-permute-start.30) | collective-permute-done | bytes 4128 | tf_op jit(solution)/shard_map/ppermute | solution.py:15
  158.3 4.7 %collective-permute-start.35 = (f32[2,16,32,1]{3,2,1,0:T(8,128)S(1)}, f32[2,16,32,1]{3,2,1,0:T(8,128)S(1)}, u32[]{:S(2)}, u32[]{:S(2)}) collective-permute-start(f32[2,16,32,1]{3,2,1,0:T(8,128)S(1)} %slice.534), channel_id=1, source_target_pairs={{0,1},{1,2},{2,3},{3,4},{4,5},{5,6},{6,7},{7,8},{8,9},{9,10},{10,1... | collective-permute-start | bytes 12296 | tf_op jit(solution)/shard_map/ppermute | solution.py:15
  163.0 4.6 %collective-permute-start.33 = (f32[2,16,1,128]{3,2,1,0:T(1,128)S(1)}, f32[2,16,1,128]{3,2,1,0:T(1,128)S(1)}, u32[]{:S(2)}, u32[]{:S(2)}) collective-permute-start(f32[2,16,1,128]{3,2,1,0:T(1,128)S(1)} %slice.530), channel_id=1, source_target_pairs={{0,32},{32,64},{64,96},{96,128},{128,160},{160,192},{192,224},{224... | collective-permute-start | bytes 49160 | tf_op jit(solution)/shard_map/ppermute | solution.py:15
  171.9 10.2 %collective-permute-done.34 = f32[2,16,32,1]{3,2,1,0:T(8,128)S(1)} collective-permute-done((f32[2,16,32,1]{3,2,1,0:T(8,128)S(1)}, f32[2,16,32,1]{3,2,1,0:T(8,128)S(1)}, u32[]{:S(2)}, u32[]{:S(2)}) %collective-permute-start.34) | collective-permute-done | bytes 4128 | tf_op jit(solution)/shard_map/ppermute | solution.py:15
  187.8 129.1 %psum.7 = f32[4,16,16]{2,1,0:T(8,128)S(1)} all-reduce(f32[4,16,16]{2,1,0:T(8,128)S(1)} %pad_maximum_fusion.3), channel_id=1, replica_groups=mesh['gx'=16,'gy'=32] {'gx','gy'}, use_global_device_ids=true, to_apply=%region_0.0 | all-reduce | flops 1024 | bytes 8192 | tf_op jit(solution)/shard_map/psum | solution.py:79
  (144 shorter events, 70.3 us)
Async XLA Ops:
  2.7 13.1 %collective-permute-start.3 = (f32[2,16,32,1]{3,2,1,0:T(8,128)S(1)}, f32[2,16,32,1]{3,2,1,0:T(8,128)S(1)}, u32[]{:S(2)}, u32[]{:S(2)}) collective-permute-start(f32[2,16,32,1]{3,2,1,0:T(8,128)S(1)} %slice.447), channel_id=1, source_target_pairs={{0,1},{1,2},{2,3},{3,4},{4,5},{5,6},{6,7},{7,8},{8,9},{9,10},{10,1... | collective-permute-start | bytes 12296 | tf_op jit(solution)/shard_map/ppermute | solution.py:15
  7.3 14.1 %collective-permute-start.1 = (f32[2,16,1,128]{3,2,1,0:T(1,128)S(1)}, f32[2,16,1,128]{3,2,1,0:T(1,128)S(1)}, u32[]{:S(2)}, u32[]{:S(2)}) collective-permute-start(f32[2,16,1,128]{3,2,1,0:T(1,128)S(1)} %slice.443), channel_id=1, source_target_pairs={{0,32},{32,64},{64,96},{96,128},{128,160},{160,192},{192,224},{224... | collective-permute-start | bytes 49160 | tf_op jit(solution)/shard_map/ppermute | solution.py:15
  22.2 11.9 %collective-permute-start.6 = (f32[2,16,32,1]{3,2,1,0:T(8,128)S(1)}, f32[2,16,32,1]{3,2,1,0:T(8,128)S(1)}, u32[]{:S(2)}, u32[]{:S(2)}) collective-permute-start(f32[2,16,32,1]{3,2,1,0:T(8,128)S(1)} %bitcast.90), channel_id=1, source_target_pairs={{1,0},{2,1},{3,2},{4,3},{5,4},{6,5},{7,6},{8,7},{9,8},{10,9},{11,1... | collective-permute-start | bytes 12296 | tf_op jit(solution)/shard_map/ppermute | solution.py:15
  24.1 15.8 %collective-permute-start.4 = (f32[2,16,1,128]{3,2,1,0:T(1,128)S(1)}, f32[2,16,1,128]{3,2,1,0:T(1,128)S(1)}, u32[]{:S(2)}, u32[]{:S(2)}) collective-permute-start(f32[2,16,1,128]{3,2,1,0:T(1,128)S(1)} %slice.451), channel_id=1, source_target_pairs={{32,0},{64,32},{96,64},{128,96},{160,128},{192,160},{224,192},{256... | collective-permute-start | bytes 49160 | tf_op jit(solution)/shard_map/ppermute | solution.py:15
  25.4 14.5 %collective-permute-start.5 = (f32[2,16,1,128]{3,2,1,0:T(1,128)S(1)}, f32[2,16,1,128]{3,2,1,0:T(1,128)S(1)}, u32[]{:S(2)}, u32[]{:S(2)}) collective-permute-start(f32[2,16,1,128]{3,2,1,0:T(1,128)S(1)} %slice.452), channel_id=1, source_target_pairs={{0,32},{32,64},{64,96},{96,128},{128,160},{160,192},{192,224},{224... | collective-permute-start | bytes 49160 | tf_op jit(solution)/shard_map/ppermute | solution.py:15
  40.8 12.2 %collective-permute-start.11 = (f32[2,16,32,1]{3,2,1,0:T(8,128)S(1)}, f32[2,16,32,1]{3,2,1,0:T(8,128)S(1)}, u32[]{:S(2)}, u32[]{:S(2)}) collective-permute-start(f32[2,16,32,1]{3,2,1,0:T(8,128)S(1)} %slice.465), channel_id=1, source_target_pairs={{0,1},{1,2},{2,3},{3,4},{4,5},{5,6},{6,7},{7,8},{8,9},{9,10},{10,1... | collective-permute-start | bytes 12296 | tf_op jit(solution)/shard_map/ppermute | solution.py:15
  45.2 14.1 %collective-permute-start.9 = (f32[2,16,1,128]{3,2,1,0:T(1,128)S(1)}, f32[2,16,1,128]{3,2,1,0:T(1,128)S(1)}, u32[]{:S(2)}, u32[]{:S(2)}) collective-permute-start(f32[2,16,1,128]{3,2,1,0:T(1,128)S(1)} %slice.461), channel_id=1, source_target_pairs={{0,32},{32,64},{64,96},{96,128},{128,160},{160,192},{192,224},{224... | collective-permute-start | bytes 49160 | tf_op jit(solution)/shard_map/ppermute | solution.py:15
  62.8 13.2 %collective-permute-start.12 = (f32[2,16,1,128]{3,2,1,0:T(1,128)S(1)}, f32[2,16,1,128]{3,2,1,0:T(1,128)S(1)}, u32[]{:S(2)}, u32[]{:S(2)}) collective-permute-start(f32[2,16,1,128]{3,2,1,0:T(1,128)S(1)} %fusion.97), channel_id=1, source_target_pairs={{32,0},{64,32},{96,64},{128,96},{160,128},{192,160},{224,192},{256... | collective-permute-start | bytes 49160 | tf_op jit(solution)/shard_map/ppermute | solution.py:15
  64.1 11.3 %collective-permute-start.14 = (f32[2,16,32,1]{3,2,1,0:T(8,128)S(1)}, f32[2,16,32,1]{3,2,1,0:T(8,128)S(1)}, u32[]{:S(2)}, u32[]{:S(2)}) collective-permute-start(f32[2,16,32,1]{3,2,1,0:T(8,128)S(1)} %fusion.13), channel_id=1, source_target_pairs={{1,0},{2,1},{3,2},{4,3},{5,4},{6,5},{7,6},{8,7},{9,8},{10,9},{11,1... | collective-permute-start | bytes 12296 | tf_op jit(solution)/shard_map/ppermute | solution.py:15
  76.8 20.1 %collective-permute-start.16 = (f32[2,16,1,128]{3,2,1,0:T(1,128)S(1)}, f32[2,16,1,128]{3,2,1,0:T(1,128)S(1)}, u32[]{:S(2)}, u32[]{:S(2)}) collective-permute-start(f32[2,16,1,128]{3,2,1,0:T(1,128)S(1)} %slice.486), channel_id=1, source_target_pairs={{32,0},{64,32},{96,64},{128,96},{160,128},{192,160},{224,192},{256... | collective-permute-start | bytes 49160 | tf_op jit(solution)/shard_map/ppermute | solution.py:15
  78.2 18.8 %collective-permute-start.17 = (f32[2,16,1,128]{3,2,1,0:T(1,128)S(1)}, f32[2,16,1,128]{3,2,1,0:T(1,128)S(1)}, u32[]{:S(2)}, u32[]{:S(2)}) collective-permute-start(f32[2,16,1,128]{3,2,1,0:T(1,128)S(1)} %slice.487), channel_id=1, source_target_pairs={{0,32},{32,64},{64,96},{96,128},{128,160},{160,192},{192,224},{224... | collective-permute-start | bytes 49160 | tf_op jit(solution)/shard_map/ppermute | solution.py:15
  84.0 11.5 %collective-permute-start.18 = (f32[2,16,32,1]{3,2,1,0:T(8,128)S(1)}, f32[2,16,32,1]{3,2,1,0:T(8,128)S(1)}, u32[]{:S(2)}, u32[]{:S(2)}) collective-permute-start(f32[2,16,32,1]{3,2,1,0:T(8,128)S(1)} %bitcast.91), channel_id=1, source_target_pairs={{1,0},{2,1},{3,2},{4,3},{5,4},{6,5},{7,6},{8,7},{9,8},{10,9},{11,1... | collective-permute-start | bytes 12296 | tf_op jit(solution)/shard_map/ppermute | solution.py:15
  97.6 21.5 %collective-permute-start.21 = (f32[2,16,1,128]{3,2,1,0:T(1,128)S(1)}, f32[2,16,1,128]{3,2,1,0:T(1,128)S(1)}, u32[]{:S(2)}, u32[]{:S(2)}) collective-permute-start(f32[2,16,1,128]{3,2,1,0:T(1,128)S(1)} %slice.496), channel_id=1, source_target_pairs={{0,32},{32,64},{64,96},{96,128},{128,160},{160,192},{192,224},{224... | collective-permute-start | bytes 49160 | tf_op jit(solution)/shard_map/ppermute | solution.py:15
  102.4 16.7 %collective-permute-start.20 = (f32[2,16,1,128]{3,2,1,0:T(1,128)S(1)}, f32[2,16,1,128]{3,2,1,0:T(1,128)S(1)}, u32[]{:S(2)}, u32[]{:S(2)}) collective-permute-start(f32[2,16,1,128]{3,2,1,0:T(1,128)S(1)} %slice.495), channel_id=1, source_target_pairs={{32,0},{64,32},{96,64},{128,96},{160,128},{192,160},{224,192},{256... | collective-permute-start | bytes 49160 | tf_op jit(solution)/shard_map/ppermute | solution.py:15
  122.6 13.2 %collective-permute-start.24 = (f32[2,16,1,128]{3,2,1,0:T(1,128)S(1)}, f32[2,16,1,128]{3,2,1,0:T(1,128)S(1)}, u32[]{:S(2)}, u32[]{:S(2)}) collective-permute-start(f32[2,16,1,128]{3,2,1,0:T(1,128)S(1)} %fusion.96), channel_id=1, source_target_pairs={{32,0},{64,32},{96,64},{128,96},{160,128},{192,160},{224,192},{256... | collective-permute-start | bytes 49160 | tf_op jit(solution)/shard_map/ppermute | solution.py:15
  123.9 10.9 %collective-permute-start.26 = (f32[2,16,32,1]{3,2,1,0:T(8,128)S(1)}, f32[2,16,32,1]{3,2,1,0:T(8,128)S(1)}, u32[]{:S(2)}, u32[]{:S(2)}) collective-permute-start(f32[2,16,32,1]{3,2,1,0:T(8,128)S(1)} %fusion.10), channel_id=1, source_target_pairs={{1,0},{2,1},{3,2},{4,3},{5,4},{6,5},{7,6},{8,7},{9,8},{10,9},{11,1... | collective-permute-start | bytes 12296 | tf_op jit(solution)/shard_map/ppermute | solution.py:15
  136.6 19.8 %collective-permute-start.28 = (f32[2,16,1,128]{3,2,1,0:T(1,128)S(1)}, f32[2,16,1,128]{3,2,1,0:T(1,128)S(1)}, u32[]{:S(2)}, u32[]{:S(2)}) collective-permute-start(f32[2,16,1,128]{3,2,1,0:T(1,128)S(1)} %slice.520), channel_id=1, source_target_pairs={{32,0},{64,32},{96,64},{128,96},{160,128},{192,160},{224,192},{256... | collective-permute-start | bytes 49160 | tf_op jit(solution)/shard_map/ppermute | solution.py:15
  137.9 18.5 %collective-permute-start.29 = (f32[2,16,1,128]{3,2,1,0:T(1,128)S(1)}, f32[2,16,1,128]{3,2,1,0:T(1,128)S(1)}, u32[]{:S(2)}, u32[]{:S(2)}) collective-permute-start(f32[2,16,1,128]{3,2,1,0:T(1,128)S(1)} %slice.521), channel_id=1, source_target_pairs={{0,32},{32,64},{64,96},{96,128},{128,160},{160,192},{192,224},{224... | collective-permute-start | bytes 49160 | tf_op jit(solution)/shard_map/ppermute | solution.py:15
  143.4 11.6 %collective-permute-start.30 = (f32[2,16,32,1]{3,2,1,0:T(8,128)S(1)}, f32[2,16,32,1]{3,2,1,0:T(8,128)}, u32[]{:S(2)}, u32[]{:S(2)}) collective-permute-start(f32[2,16,32,1]{3,2,1,0:T(8,128)S(1)} %bitcast.89), channel_id=1, source_target_pairs={{1,0},{2,1},{3,2},{4,3},{5,4},{6,5},{7,6},{8,7},{9,8},{10,9},{11,1... | collective-permute-start | bytes 12296 | tf_op jit(solution)/shard_map/ppermute | solution.py:15
  145.6 10.8 %collective-permute-start.31 = (f32[2,16,32,1]{3,2,1,0:T(8,128)S(1)}, f32[2,16,32,1]{3,2,1,0:T(8,128)}, u32[]{:S(2)}, u32[]{:S(2)}) collective-permute-start(f32[2,16,32,1]{3,2,1,0:T(8,128)S(1)} %slice.525), channel_id=1, source_target_pairs={{0,1},{1,2},{2,3},{3,4},{4,5},{5,6},{6,7},{7,8},{8,9},{9,10},{10,1... | collective-permute-start | bytes 12296 | tf_op jit(solution)/shard_map/ppermute | solution.py:15
  158.3 13.6 %collective-permute-start.35 = (f32[2,16,32,1]{3,2,1,0:T(8,128)S(1)}, f32[2,16,32,1]{3,2,1,0:T(8,128)S(1)}, u32[]{:S(2)}, u32[]{:S(2)}) collective-permute-start(f32[2,16,32,1]{3,2,1,0:T(8,128)S(1)} %slice.534), channel_id=1, source_target_pairs={{0,1},{1,2},{2,3},{3,4},{4,5},{5,6},{6,7},{7,8},{8,9},{9,10},{10,1... | collective-permute-start | bytes 12296 | tf_op jit(solution)/shard_map/ppermute | solution.py:15
  163.0 19.1 %collective-permute-start.33 = (f32[2,16,1,128]{3,2,1,0:T(1,128)S(1)}, f32[2,16,1,128]{3,2,1,0:T(1,128)S(1)}, u32[]{:S(2)}, u32[]{:S(2)}) collective-permute-start(f32[2,16,1,128]{3,2,1,0:T(1,128)S(1)} %slice.530), channel_id=1, source_target_pairs={{0,32},{32,64},{64,96},{96,128},{128,160},{160,192},{192,224},{224... | collective-permute-start | bytes 49160 | tf_op jit(solution)/shard_map/ppermute | solution.py:15
  167.6 14.5 %collective-permute-start.34 = (f32[2,16,32,1]{3,2,1,0:T(8,128)S(1)}, f32[2,16,32,1]{3,2,1,0:T(8,128)S(1)}, u32[]{:S(2)}, u32[]{:S(2)}) collective-permute-start(f32[2,16,32,1]{3,2,1,0:T(8,128)S(1)} %bitcast.87), channel_id=1, source_target_pairs={{1,0},{2,1},{3,2},{4,3},{5,4},{6,5},{7,6},{8,7},{9,8},{10,9},{11,1... | collective-permute-start | bytes 12296 | tf_op jit(solution)/shard_map/ppermute | solution.py:15
  169.5 12.6 %collective-permute-start.32 = (f32[2,16,1,128]{3,2,1,0:T(1,128)S(1)}, f32[2,16,1,128]{3,2,1,0:T(1,128)S(1)}, u32[]{:S(2)}, u32[]{:S(2)}) collective-permute-start(f32[2,16,1,128]{3,2,1,0:T(1,128)S(1)} %slice.529), channel_id=1, source_target_pairs={{32,0},{64,32},{96,64},{128,96},{160,128},{192,160},{224,192},{256... | collective-permute-start | bytes 49160 | tf_op jit(solution)/shard_map/ppermute | solution.py:15
  (16 other events, 136.3 us)
where the time goes:
time: 319 us; the launch traced here: 317 us
  blocking collectives  129 us (40%)
  starting transfers between devices  111 us (35%)
  waiting for transfers between devices  49 us (15%)
  other arithmetic  19 us (6%)
  local copies, waits for them, and re-layouts  4.54 us (1%)
    psum x1, blocking collectives, on_device(): summed = lax.psum(partial_sums, ('gx', 'gy'))  129 us
    ppermute x36, starting transfers between devices, passed_along(): return lax.ppermute(array, axis, pairs)  111 us
    ppermute x36, waiting for transfers between devices, passed_along(): return lax.ppermute(array, axis, pairs)  49 us
  transfers between devices with their start and end apart: 36, of which 13 were waited for; matrix products, arithmetic and copies ran while one was open for 1% of the time, Pallas kernels for 0%

commit v1 on v0

v1 whole, which is shorter than its diff:
```python
import jax
import jax.numpy as jnp
from jax import lax
from jax.experimental import pallas as pl
from jax.experimental.pallas import tpu as pltpu
from jax.sharding import PartitionSpec as P

STEPS = 3
DEPTH = 3 * STEPS
ROWS, COLS, FIELDS = 32, 128, 32
GROUPS = 4
SPAN = COLS // GROUPS
TALL = ROWS + 2 * DEPTH
TALL_PAD = 56
TILE = 8 * (GROUPS + 1)
THIRD = 17
ROW_MSG = DEPTH * FIELDS + 3 * 16
COL_MSG = 8 * THIRD + TALL_PAD

f32 = jnp.float32


def lanes_of(shape):
    return lax.broadcasted_iota(jnp.int32, shape, len(shape) - 1)


def pack_rows(state, potential, bonds, wave, masks, to_prev, to_next):
    last_x = lax.axis_index("gx") == lax.axis_size("gx") - 1
    last_y = lax.axis_index("gy") == lax.axis_size("gy") - 1
    for f in range(FIELDS):
        own = state[f].astype(f32)
        wave[pl.ds(f, ROWS, stride=FIELDS), :] = pltpu.roll(own, SPAN * (f // 8), 1) if f >= 8 else own
    row = lax.broadcasted_iota(jnp.int32, (ROWS, COLS), 0)
    lane = lanes_of((ROWS, COLS))
    masks[0] = potential[...]
    masks[1] = jnp.where(jnp.logical_and(last_x, row == ROWS - 1), 0.0, bonds[0].astype(f32))
    masks[2] = jnp.where(jnp.logical_and(last_y, lane == COLS - 1), 0.0, bonds[1].astype(f32))
    many = DEPTH * FIELDS
    to_prev[:many] = wave[:many]
    to_next[:many] = wave[ROWS * FIELDS - many :]
    for m in range(3):
        to_prev[many + 16 * m : many + 16 * m + 16] = masks[m, :16]
        to_next[many + 16 * m : many + 16 * m + 16] = masks[m, ROWS - 16 :]


def pack_columns(wave, masks, above, below, rotated, to_left, to_right):
    many = DEPTH * FIELDS
    lane = lanes_of((8, COLS))
    inner = lane % SPAN
    block = lane // SPAN

    def merged(parts, first):
        out = parts[first % GROUPS]
        for b in range(1, GROUPS):
            out = jnp.where(block[:1] == b, parts[(b + first) % GROUPS], out)
        return out

    def packed_left(a, b, c):
        return jnp.where(inner[:1] < 9, a, jnp.where(inner[:1] < 18, pltpu.roll(b, 9, 1), pltpu.roll(c, 18, 1)))

    def packed_right(a, b, c):
        back = lambda v, by: pltpu.roll(v, COLS - by, 1)
        return jnp.where(inner[:1] >= SPAN - 9, a, jnp.where(inner[:1] >= SPAN - 18, back(b, 9), back(c, 18)))

    lefts, rights = [], []
    for i in range(TALL):
        if i < DEPTH:
            ref, at = above, i * FIELDS
        elif i < DEPTH + ROWS:
            ref, at = wave, (i - DEPTH) * FIELDS
        else:
            ref, at = below, (i - DEPTH - ROWS) * FIELDS
        parts = [ref[at + 8 * k : at + 8 * k + 8] for k in range(GROUPS)]
        lefts.append(merged(parts, 0))
        rights.append(merged(parts, 1))
    lefts.append(lefts[0])
    rights.append(rights[0])
    for t in range(THIRD):
        to_left[8 * t : 8 * t + 8] = packed_left(lefts[t], lefts[t + THIRD], lefts[t + 2 * THIRD])
        to_right[8 * t : 8 * t + 8] = packed_right(rights[t], rights[t + THIRD], rights[t + 2 * THIRD])
    left_masks, right_masks = [], []
    for m in range(3):
        at = many + 16 * m
        tall = jnp.concatenate(
            [
                above[at + 16 - DEPTH : at + 16],
                masks[m],
                below[at : at + DEPTH],
                jnp.zeros((TALL_PAD - TALL, COLS), f32),
            ],
            axis=0,
        )
        parts = [pltpu.roll(tall, SPAN * k, 1) if k else tall for k in range(GROUPS)]
        for k in range(GROUPS):
            rotated[m, k] = parts[k]
        left_masks.append(merged(parts, 0))
        right_masks.append(merged(parts, 1))
    to_left[8 * THIRD :] = packed_left(*left_masks)
    to_right[8 * THIRD :] = packed_right(*right_masks)


def evolve(
    coeffs, boundary, phase, wave, above, below, rotated, from_right, from_left, evolved, shares,
    cur, one, two, spread, halo_masks, flat, cells,
):
    lane = lanes_of((8, COLS))
    near = (lane % SPAN) < SPAN // 2
    near_row = near[:1]

    def joined(right, left, u):
        if u:
            right = pltpu.roll(right, COLS - 9 * u, 1)
            left = pltpu.roll(left, 9 * u, 1)
        return jnp.where(near_row, right, left)

    for i in range(TALL):
        if i < DEPTH:
            ref, at = above, i * FIELDS
        elif i < DEPTH + ROWS:
            ref, at = wave, (i - DEPTH) * FIELDS
        else:
            ref, at = below, (i - DEPTH - ROWS) * FIELDS
        cur[TILE * i : TILE * i + FIELDS] = ref[at : at + FIELDS]
        t, u = i % THIRD, i // THIRD
        cur[TILE * i + FIELDS : TILE * i + TILE] = joined(
            from_right[8 * t : 8 * t + 8], from_left[8 * t : 8 * t + 8], u
        )
    for m in range(3):
        halo_masks[m] = joined(from_right[8 * THIRD :], from_left[8 * THIRD :], m)
        for i in range(TALL):
            for k in range(GROUPS):
                spread[m, TILE * i + 8 * k : TILE * i + 8 * k + 8] = jnp.broadcast_to(rotated[m, k, i : i + 1], (8, COLS))
            spread[m, TILE * i + FIELDS : TILE * i + TILE] = jnp.broadcast_to(halo_masks[m, i : i + 1], (8, COLS))

    lane_main = lanes_of((FIELDS, COLS))
    group_main = lax.broadcasted_iota(jnp.int32, (FIELDS, COLS), 0) // 8
    seam_left = lane_main == SPAN * group_main
    seam_right = lane_main == (SPAN * group_main + COLS - 1) % COLS
    left_at = [lane == SPAN * k for k in range(GROUPS)]
    right_at = [lane == (SPAN * k + COLS - 1) % COLS for k in range(GROUPS)]

    def sewn(shifted, seam, at):
        main, rim = shifted[:FIELDS], shifted[FIELDS:]
        over = jnp.where(seam, jnp.concatenate([rim] * GROUPS, axis=0), main)
        for k in range(GROUPS):
            rim = jnp.where(at[k], main[8 * k : 8 * k + 8], rim)
        return jnp.concatenate([over, rim], axis=0)

    def row_of(ref, i):
        return ref[TILE * i : TILE * i + TILE]

    def hamilton(source, first, after, finish):
        here = row_of(source, first)
        handed = row_of(spread.at[1], first - 1) * row_of(source, first - 1)
        for i in range(first, after):
            following = row_of(source, i + 1)
            pot, down, side = (row_of(spread.at[m], i) for m in range(3))
            right = sewn(pltpu.roll(here, COLS - 1, 1), seam_right, right_at)
            left = sewn(pltpu.roll(side * here, 1, 1), seam_left, left_at)
            hop = (down * following + handed) + (side * right + left)
            finish(i, pot * here - hop)
            handed = down * here
            here = following

    c0, c1, c2, c3 = (coeffs[k] for k in range(4))
    e3 = 4.0 * c3 / 125.0
    scale = e3 * e3 * e3
    one_vec = jnp.ones((1, COLS), f32)
    per = 1.0 / (one_vec * e3)
    a0 = one_vec * (c0 + c2) * per
    a1 = one_vec * ((c1 + 3.0 * c3) / 5.0) * per
    a2 = one_vec * (2.0 * c2 / 25.0) * per

    def put(ref, i, value):
        ref[TILE * i : TILE * i + TILE] = value

    def second(i, value):
        start = row_of(cur, i)
        put(two, i, a1 * start - value)
        put(cur, i, a0 * start - a2 * value)

    half = FIELDS // 2
    real_lanes = (lane + SPAN // 2) % COLS < COLS // 2

    def third(i, value):
        turned = pltpu.roll(value, COLS // 2, 1)
        start = row_of(cur, i)
        re = start[:half] + turned[half:FIELDS]
        im = start[half:FIELDS] - turned[:half]
        rim = start[FIELDS:] + jnp.where(real_lanes, turned[FIELDS:], -turned[FIELDS:])
        put(cur, i, jnp.concatenate([re, im, rim], axis=0))

    for step in range(STEPS):
        d = 3 * step
        hamilton(cur, d + 1, TALL - d - 1, lambda i, value: put(one, i, value))
        hamilton(one, d + 2, TALL - d - 2, second)
        hamilton(two, d + 3, TALL - d - 3, third)

    for r in range(ROWS):
        at = TILE * (r + DEPTH)
        for k in range(GROUPS):
            part = cur[at + 8 * k : at + 8 * k + 8] * scale
            if k:
                part = pltpu.roll(part, COLS - SPAN * k, 1)
            cells[r * FIELDS + 8 * k : r * FIELDS + 8 * k + 8] = part
        flat[:, COLS * r : COLS * r + COLS] = cells[r * FIELDS : r * FIELDS + FIELDS].astype(jnp.bfloat16)
    for f in range(FIELDS):
        evolved[f] = cells[pl.ds(f, ROWS, stride=FIELDS), :].astype(jnp.bfloat16)

    first_col = lax.axis_index("gy") * COLS
    inside = (lanes_of((1, COLS)) + first_col >= boundary[0]).astype(f32).astype(jnp.bfloat16)
    amps = flat[...]
    amps_right = jnp.concatenate([amps[:, COLS * r : COLS * r + COLS] * inside for r in range(ROWS)], axis=1)
    contract = (((1,), (1,)), ((), ()))
    total = lax.dot_general(amps, amps, contract, preferred_element_type=f32)
    right = lax.dot_general(amps, amps_right, contract, preferred_element_type=f32)
    n = half
    total_re = total[:n, :n] + total[n:, n:]
    total_im = total[:n, n:] - total[n:, :n]
    right_re = right[:n, :n] + right[n:, n:]
    right_im = right[:n, n:] - right[n:, :n]
    cosine, sine, count = phase[0], phase[1], phase[2]
    over_re = (total_re + cosine * right_re - sine * right_im) * count
    over_im = (total_im + cosine * right_im + sine * right_re) * count
    wide = jnp.concatenate([over_re, over_im], axis=0)
    tile = jnp.concatenate([wide[8 * k : 8 * k + 8] for k in range(4)] + [jnp.zeros((8, COLS - 4 * n), f32)], axis=1)
    for p in range(shares.shape[0]):
        shares[p] = tile


def add_and_copy(parts, shares):
    total = jnp.sum(parts[...], axis=0)
    for p in range(shares.shape[0]):
        shares[p] = total


def add_and_open(parts, out):
    total = jnp.sum(parts[...], axis=0)
    n = out.shape[-1]
    for k in range(4):
        out[k // 2, 8 * (k % 2) : 8 * (k % 2) + 8] = total[:, n * k : n * k + n]


def whole():
    return pl.BlockSpec(memory_space=pltpu.VMEM)


def scalars():
    return pl.BlockSpec(memory_space=pltpu.SMEM)


def call(kernel, outs, in_specs, scratch=(), limit=None):
    return pl.pallas_call(
        kernel,
        out_shape=[jax.ShapeDtypeStruct(s, d) for s, d in outs],
        in_specs=in_specs,
        out_specs=[whole()] * len(outs),
        scratch_shapes=list(scratch),
        compiler_params=pltpu.CompilerParams(vmem_limit_bytes=limit) if limit else None,
    )


def moved(array, axis, by):
    peers = lax.axis_size(axis)
    return lax.ppermute(array, axis, [(i, (i + by) % peers) for i in range(peers)])


def on_device(state, potential, bonds, coeffs, boundary, counting):
    norbit = state.shape[1]
    peers_x, peers_y = lax.axis_size("gx"), lax.axis_size("gy")
    count = float(ROWS * COLS * peers_x * peers_y)
    phase = jnp.stack([jnp.cos(counting[0]) - 1.0, jnp.sin(counting[0]), jnp.float32(1.0 / count)])
    wave, masks, to_prev, to_next = call(
        pack_rows,
        [((ROWS * FIELDS, COLS), f32), ((3, ROWS, COLS), f32), ((ROW_MSG, COLS), f32), ((ROW_MSG, COLS), f32)],
        [whole()] * 3,
    )(state.reshape(FIELDS, ROWS, COLS), potential, bonds)
    above = moved(to_next, "gx", 1)
    below = moved(to_prev, "gx", -1)
    rotated, to_left, to_right = call(
        pack_columns,
        [((3, GROUPS, TALL_PAD, COLS), f32), ((COL_MSG, COLS), f32), ((COL_MSG, COLS), f32)],
        [whole()] * 4,
    )(wave, masks, above, below)
    from_right = moved(to_left, "gy", -1)
    from_left = moved(to_right, "gy", 1)
    evolved, shares = call(
        evolve,
        [((FIELDS, ROWS, COLS), jnp.bfloat16), ((peers_y, 8, COLS), f32)],
        [scalars()] * 3 + [whole()] * 6,
        [
            pltpu.VMEM((TILE * TALL, COLS), f32),
            pltpu.VMEM((TILE * TALL, COLS), f32),
            pltpu.VMEM((TILE * TALL, COLS), f32),
            pltpu.VMEM((3, TILE * TALL, COLS), f32),
            pltpu.VMEM((3, TALL_PAD, COLS), f32),
            pltpu.VMEM((FIELDS, ROWS * COLS), jnp.bfloat16),
            pltpu.VMEM((ROWS * FIELDS, COLS), f32),
        ],
        limit=40 * 1024 * 1024,
    )(coeffs, boundary, phase, wave, above, below, rotated, from_right, from_left)
    parts = lax.all_to_all(shares, "gy", 0, 0, tiled=True)
    (shares,) = call(add_and_copy, [((peers_x, 8, COLS), f32)], [whole()])(parts)
    parts = lax.all_to_all(shares, "gx", 0, 0, tiled=True)
    (over,) = call(add_and_open, [((2, norbit, norbit), f32)], [whole()])(parts)
    return evolved.reshape(state.shape), over


def solution(mesh):
    return jax.shard_map(
        on_device,
        mesh=mesh,
        in_specs=(P(None, None, "gx", "gy"), P("gx", "gy"), P(None, "gx", "gy"), P(), P(), P()),
        out_specs=(P(None, None, "gx", "gy"), P()),
        check_vma=False,
    )
```

time: 319 us -> 91.1 us (0.29)
  blocking collectives: 129 us -> 38.3 us
  starting transfers between devices: 111 us -> 20.5 us
  waiting for transfers between devices: 49 us -> 5.38 us
  Pallas kernels: 0 us -> 20.6 us
  other arithmetic: 19 us -> 0.08 us
    psum x1 -> x0, blocking collectives: 129 us -> none  [on_device(): summed = lax.psum(partial_sums, ('gx', 'gy'))]
    ppermute x36 -> x4, starting transfers between devices: 111 us -> 20.5 us  [moved(): lax.ppermute(array, axis, [(i, (i + by) % peers) for i in range(peers)])]
    ppermute x36 -> x4, waiting for transfers between devices: 49 us -> 5.38 us  [moved(): lax.ppermute(array, axis, [(i, (i + by) % peers) for i in range(peers)])]
    all_to_all x0 -> x2, blocking collectives: none -> 38.3 us  [the longest x1 20.7 us: on_device(): parts = lax.all_to_all(shares, 'gx', 0, 0, tiled=True)]
    pallas_call x0 -> x5, Pallas kernels: none -> 20.6 us  [the longest x1 13 us: on_device(): call(evolve, [((FIELDS, ROWS, COLS), jnp.bfloat16), ((peers_y, 8, COLS),...]
    sub x5 -> x0, other arithmetic: 7.15 us -> none  [the longest x2 5.49 us: on_device(): coeffs[0] * term_zero[0] + coeffs[1] * term_one[1] - coeffs[2] * term_two[0]]
    mul x17 -> x0, other arithmetic: 6.26 us -> none  [the longest x6 4.45 us: hamilton(): moved_col = mask_col * wave]
    another operation x12 -> x1, other arithmetic: 4.74 us -> 0.08 us  [on_device(): jnp.stack([jnp.cos(counting[0]) - 1.0, jnp.sin(counting[0]), jnp.float32(...]
  transfers between devices with their start and end apart: 36 -> 4, of which waited for: 13 -> 4; matrix products, arithmetic and copies ran while one was open for 1% -> 0% of each run, Pallas kernels for 0% -> 0%
where the time goes in v1:
time: 91.1 us; the launch traced here: 90.6 us
  blocking collectives  38.3 us (42%)
  Pallas kernels  20.6 us (23%)
  starting transfers between devices  20.5 us (23%)
  waiting for transfers between devices  5.38 us (6%)
  local copies, waits for them, and re-layouts  3.49 us (4%)
  between operations  2.12 us (2%)
    all_to_all x1, blocking collectives, on_device(): parts = lax.all_to_all(shares, 'gx', 0, 0, tiled=True)  20.7 us
    ppermute x4, starting transfers between devices, moved(): lax.ppermute(array, axis, [(i, (i + by) % peers) for i in range(peers)])  20.5 us
    all_to_all x1, blocking collectives, on_device(): parts = lax.all_to_all(shares, 'gy', 0, 0, tiled=True)  17.7 us
    pallas_call x1, Pallas kernels, on_device(): call(evolve, [((FIELDS, ROWS, COLS), jnp.bfloat16), ((peers_y, 8, COLS),...  13 us
    ppermute x4, waiting for transfers between devices, moved(): lax.ppermute(array, axis, [(i, (i + by) % peers) for i in range(peers)])  5.38 us
    unnamed x14, local copies, waits for them, and re-layouts  3.49 us
    pallas_call x1, Pallas kernels, on_device(): call(pack_rows, [((ROWS * FIELDS, COLS), f32), ((3, ROWS, COLS), f32), ((...  2.38 us
    pallas_call x1, Pallas kernels, on_device(): call(pack_columns, [((3, GROUPS, TALL_PAD, COLS), f32), ((COL_MSG, COLS),...  2.18 us
  transfers between devices with their start and end apart: 4, of which 4 were waited for; matrix products, arithmetic and copies ran while one was open for 0% of the time, Pallas kernels for 0%

profile of v1, /device:TPU:1, one launch (start us, length us, event | category | flops | bytes accessed | tf_op | source)
XLA Modules:
  0.0 90.6 jit_solution(3818934731863863513)
XLA Ops:
  0.6 2.4 %shard_map.77 = (f32[1024,128]{1,0:T(8,128)}, f32[3,32,128]{2,1,0:T(8,128)}, f32[336,128]{1,0:T(8,128)}, f32[336,128]{1,0:T(8,128)}) custom-call(bf16[32,32,128]{2,1,0:T(8,128)(2,1)} %bitcast.2, f32[32,128]{1,0:T(8,128)} %potential.1, s32[2,32,128]{2,1,0:T(8,128)} %bonds.1), custom_call_target="tpu_custom_call" | custom-call | tf_op jit(solution)/shard_map/pallas_call | solution.py:273
  3.0 0.0 copy-start
  3.0 4.5 %collective-permute-start = (f32[336,128]{1,0:T(8,128)}, f32[336,128]{1,0:T(8,128)S(1)}, u32[]{:S(2)}, u32[]{:S(2)}) collective-permute-start(f32[336,128]{1,0:T(8,128)} %get-tuple-element.12), channel_id=1, source_target_pairs={{0,32},{32,64},{64,96},{96,128},{128,160},{160,192},{192,224},{224... | collective-permute-start | bytes 516104 | tf_op jit(solution)/shard_map/ppermute | solution.py:265
  7.5 9.5 %collective-permute-start.1 = (f32[336,128]{1,0:T(8,128)}, f32[336,128]{1,0:T(8,128)S(1)}, u32[]{:S(2)}, u32[]{:S(2)}) collective-permute-start(f32[336,128]{1,0:T(8,128)} %get-tuple-element.13), channel_id=1, source_target_pairs={{0,480},{32,0},{64,32},{96,64},{128,96},{160,128},{192,160},{224,1... | collective-permute-start | bytes 516104 | tf_op jit(solution)/shard_map/ppermute | solution.py:265
  18.5 0.9 %collective-permute-done.above = f32[336,128]{1,0:T(8,128)S(1)} collective-permute-done((f32[336,128]{1,0:T(8,128)}, f32[336,128]{1,0:T(8,128)S(1)}, u32[]{:S(2)}, u32[]{:S(2)}) %collective-permute-start) | collective-permute-done | bytes 172064 | tf_op jit(solution)/shard_map/ppermute | solution.py:265
  19.4 1.0 %collective-permute-done.1.below = f32[336,128]{1,0:T(8,128)S(1)} collective-permute-done((f32[336,128]{1,0:T(8,128)}, f32[336,128]{1,0:T(8,128)S(1)}, u32[]{:S(2)}, u32[]{:S(2)}) %collective-permute-start.1) | collective-permute-done | bytes 172064 | tf_op jit(solution)/shard_map/ppermute | solution.py:265
  20.4 0.0 copy-done.1
  20.4 0.7 copy-done.3
  21.0 2.2 %shard_map.78 = (f32[3,4,56,128]{3,2,1,0:T(8,128)}, f32[192,128]{1,0:T(8,128)}, f32[192,128]{1,0:T(8,128)}) custom-call(f32[1024,128]{1,0:T(8,128)} %get-tuple-element.11.wave, f32[3,32,128]{2,1,0:T(8,128)} %get-tuple-element.14.masks, f32[336,128]{1,0:T(8,128)} %copy-done.1, f32[336,128]{1,0:T(8,128)} %copy-done.3), custom_call_target="tpu_custom_call" | custom-call | tf_op jit(solution)/shard_map/pallas_call | solution.py:280
  23.2 3.4 %collective-permute-start.2 = (f32[192,128]{1,0:T(8,128)}, f32[192,128]{1,0:T(8,128)S(1)}, u32[]{:S(2)}, u32[]{:S(2)}) collective-permute-start(f32[192,128]{1,0:T(8,128)} %get-tuple-element.16), channel_id=1, source_target_pairs={{0,31},{1,0},{2,1},{3,2},{4,3},{5,4},{6,5},{7,6},{8,7},{9,8},{10,9... | collective-permute-start | bytes 294920 | tf_op jit(solution)/shard_map/ppermute | solution.py:265
  26.7 3.1 %collective-permute-start.3 = (f32[192,128]{1,0:T(8,128)}, f32[192,128]{1,0:T(8,128)S(1)}, u32[]{:S(2)}, u32[]{:S(2)}) collective-permute-start(f32[192,128]{1,0:T(8,128)} %get-tuple-element.17), channel_id=1, source_target_pairs={{0,1},{1,2},{2,3},{3,4},{4,5},{5,6},{6,7},{7,8},{8,9},{9,10},{10,1... | collective-permute-start | bytes 294920 | tf_op jit(solution)/shard_map/ppermute | solution.py:265
  29.8 0.1 pad_maximum_fusion.phase
  29.9 0.5 collective-permute-done.2.from_right
  30.3 3.0 %collective-permute-done.3.from_left = f32[192,128]{1,0:T(8,128)S(1)} collective-permute-done((f32[192,128]{1,0:T(8,128)}, f32[192,128]{1,0:T(8,128)S(1)}, u32[]{:S(2)}, u32[]{:S(2)}) %collective-permute-start.3) | collective-permute-done | bytes 98336 | tf_op jit(solution)/shard_map/ppermute | solution.py:265
  33.3 0.0 copy-done
  33.3 0.0 copy-done.6
  33.4 0.9 %copy-done.2 = f32[336,128]{1,0:T(8,128)S(1)} copy-done((f32[336,128]{1,0:T(8,128)S(1)}, f32[336,128]{1,0:T(8,128)}, u32[]{:S(2)}) %copy-start.2) | copy-done | bytes 172056
  34.3 0.9 %copy-done.4 = f32[336,128]{1,0:T(8,128)S(1)} copy-done((f32[336,128]{1,0:T(8,128)S(1)}, f32[336,128]{1,0:T(8,128)}, u32[]{:S(2)}) %copy-start.4) | copy-done | bytes 172056
  35.2 1.0 %copy-done.5 = f32[3,4,56,128]{3,2,1,0:T(8,128)S(1)} copy-done((f32[3,4,56,128]{3,2,1,0:T(8,128)S(1)}, f32[3,4,56,128]{3,2,1,0:T(8,128)}, u32[]{:S(2)}) %copy-start.5) | copy-done | bytes 344088
  36.2 13.0 %shard_map.79 = (bf16[32,32,128]{2,1,0:T(8,128)(2,1)}, f32[32,8,128]{2,1,0:T(8,128)S(1)}) custom-call(f32[4]{0:T(128)S(1)} %copy-done.6, s32[1]{0:T(128)S(6)} %copy.8.boundary, f32[3]{0:T(128)S(1)} %pad_maximum_fusion.phase, f32[1024,128]{1,0:T(8,128)S(1)} %copy-done, f32[336,128]{1,0:T(8,128)S(1)} %copy-done.2, f32[336,128]{1,0:T(8,128)S(1)} %copy-done.4, ...), custom_call_target="tpu_custom_call" | custom-call | tf_op jit(solution)/shard_map/pallas_call | solution.py:287
  49.1 17.7 %all_to_all.10.parts = f32[32,8,128]{2,1,0:T(8,128)} all-to-all(f32[32,8,128]{2,1,0:T(8,128)S(1)} %get-tuple-element.19), channel_id=1, replica_groups=mesh['gx'=16,'gy'=32] {'gy'}, dimensions={0} | all-to-all | bytes 262144 | tf_op jit(solution)/shard_map/all_to_all | solution.py:302
  66.8 1.6 %shard_map.80 = f32[16,8,128]{2,1,0:T(8,128)} custom-call(f32[32,8,128]{2,1,0:T(8,128)} %all_to_all.10.parts), custom_call_target="tpu_custom_call" | custom-call | tf_op jit(solution)/shard_map/pallas_call | solution.py:303
  68.4 20.7 %all_to_all.11.parts = f32[16,8,128]{2,1,0:T(8,128)} all-to-all(f32[16,8,128]{2,1,0:T(8,128)} %shard_map.80), channel_id=1, replica_groups=mesh['gx'=16,'gy'=32] {'gx'}, dimensions={0} | all-to-all | bytes 131072 | tf_op jit(solution)/shard_map/all_to_all | solution.py:304
  89.0 1.5 %shard_map.81 = f32[2,16,16]{2,1,0:T(8,128)} custom-call(f32[16,8,128]{2,1,0:T(8,128)} %all_to_all.11.parts), custom_call_target="tpu_custom_call" | custom-call | tf_op jit(solution)/shard_map/pallas_call | solution.py:305
  (6 shorter events, 0.0 us)
Async XLA Ops:
  3.0 30.3 %copy-start = (f32[1024,128]{1,0:T(8,128)S(1)}, f32[1024,128]{1,0:T(8,128)}, u32[]{:S(2)}) copy-start(f32[1024,128]{1,0:T(8,128)} %get-tuple-element.11.wave) | copy-start | bytes 1572868
  3.0 16.4 %collective-permute-start = (f32[336,128]{1,0:T(8,128)}, f32[336,128]{1,0:T(8,128)S(1)}, u32[]{:S(2)}, u32[]{:S(2)}) collective-permute-start(f32[336,128]{1,0:T(8,128)} %get-tuple-element.12), channel_id=1, source_target_pairs={{0,32},{32,64},{64,96},{96,128},{128,160},{160,192},{192,224},{224... | collective-permute-start | bytes 516104 | tf_op jit(solution)/shard_map/ppermute | solution.py:265
  7.5 12.8 %collective-permute-start.1 = (f32[336,128]{1,0:T(8,128)}, f32[336,128]{1,0:T(8,128)S(1)}, u32[]{:S(2)}, u32[]{:S(2)}) collective-permute-start(f32[336,128]{1,0:T(8,128)} %get-tuple-element.13), channel_id=1, source_target_pairs={{0,480},{32,0},{64,32},{96,64},{128,96},{160,128},{192,160},{224,1... | collective-permute-start | bytes 516104 | tf_op jit(solution)/shard_map/ppermute | solution.py:265
  19.4 1.0 %copy-start.1 = (f32[336,128]{1,0:T(8,128)}, f32[336,128]{1,0:T(8,128)S(1)}, u32[]{:S(2)}) copy-start(f32[336,128]{1,0:T(8,128)S(1)} %collective-permute-done.above) | copy-start | bytes 516100
  20.4 0.7 copy-start.3
  23.2 7.1 %collective-permute-start.2 = (f32[192,128]{1,0:T(8,128)}, f32[192,128]{1,0:T(8,128)S(1)}, u32[]{:S(2)}, u32[]{:S(2)}) collective-permute-start(f32[192,128]{1,0:T(8,128)} %get-tuple-element.16), channel_id=1, source_target_pairs={{0,31},{1,0},{2,1},{3,2},{4,3},{5,4},{6,5},{7,6},{8,7},{9,8},{10,9... | collective-permute-start | bytes 294920 | tf_op jit(solution)/shard_map/ppermute | solution.py:265
  26.7 6.7 %collective-permute-start.3 = (f32[192,128]{1,0:T(8,128)}, f32[192,128]{1,0:T(8,128)S(1)}, u32[]{:S(2)}, u32[]{:S(2)}) collective-permute-start(f32[192,128]{1,0:T(8,128)} %get-tuple-element.17), channel_id=1, source_target_pairs={{0,1},{1,2},{2,3},{3,4},{4,5},{5,6},{6,7},{7,8},{8,9},{9,10},{10,1... | collective-permute-start | bytes 294920 | tf_op jit(solution)/shard_map/ppermute | solution.py:265
  29.8 3.5 %copy-start.6 = (f32[4]{0:T(128)S(1)}, f32[4]{0:T(128)}, u32[]{:S(2)}) copy-start(f32[4]{0:T(128)} %coeffs.1) | copy-start | bytes 52
  33.4 0.9 %copy-start.2 = (f32[336,128]{1,0:T(8,128)S(1)}, f32[336,128]{1,0:T(8,128)}, u32[]{:S(2)}) copy-start(f32[336,128]{1,0:T(8,128)} %copy-done.1) | copy-start | bytes 516100
  34.3 0.9 %copy-start.4 = (f32[336,128]{1,0:T(8,128)S(1)}, f32[336,128]{1,0:T(8,128)}, u32[]{:S(2)}) copy-start(f32[336,128]{1,0:T(8,128)} %copy-done.3) | copy-start | bytes 516100
  35.2 1.0 %copy-start.5 = (f32[3,4,56,128]{3,2,1,0:T(8,128)S(1)}, f32[3,4,56,128]{3,2,1,0:T(8,128)}, u32[]{:S(2)}) copy-start(f32[3,4,56,128]{3,2,1,0:T(8,128)} %get-tuple-element.15.rotated) | copy-start | bytes 1032196

commit v2 on v0

v2 whole, which is shorter than its diff:
```python
import jax
import jax.numpy as jnp
from jax import lax
from jax.experimental import pallas as pl
from jax.experimental.pallas import tpu as pltpu
from jax.sharding import PartitionSpec as P

STEPS = 3
DEPTH = 3 * STEPS
ROWS, COLS, FIELDS = 32, 128, 32
GROUPS = 4
HALF = COLS // 2
TALL = ROWS + 2 * DEPTH
TALL_PAD = 56
BATCH = 16
CHUNK = 8
PIECES = 7
PLACES = 8
EDGE = DEPTH * FIELDS
THIN = 16
ROW_MSG = EDGE + 3 * 16
COL_MSG = THIN * PLACES + TALL_PAD
MIB = 1024 * 1024

f32 = jnp.float32


def lanes():
    return lax.broadcasted_iota(jnp.int32, (1, COLS), 1)


def inner_lanes():
    return lanes() & (HALF - 1)


def turn(value, by):
    by = by % COLS
    return pltpu.roll(value, by, value.ndim - 1) if by else value


def ends(a, b):
    low = lanes() < HALF
    return jnp.where(low, a, turn(b, HALF)), jnp.where(low, turn(a, HALF), b)


def own_strip(head, tail):
    return jnp.where(inner_lanes() < HALF // 2, turn(head, DEPTH), turn(tail, -DEPTH))


def packed(parts, first):
    out = turn(parts[0], -first)
    for u in range(1, len(parts)):
        out = jnp.where(inner_lanes() < DEPTH * u, out, turn(parts[u], DEPTH * u - first))
    return out


def join(from_left, own, from_right, u):
    inner = inner_lanes()
    left = turn(from_left, -DEPTH * u)
    right = turn(from_right, HALF - DEPTH - DEPTH * u)
    return jnp.where(inner < DEPTH, left, jnp.where(inner < HALF - DEPTH, own, right))


def ends_of(ref, at):
    groups = [ref[at + 8 * g : at + 8 * g + 8] for g in range(GROUPS)]
    both = [ends(groups[2 * p], groups[2 * p + 1]) for p in range(2)]
    return tuple(jnp.concatenate([pair[k] for pair in both], axis=0) for k in range(2))


def fetched(sources, targets, sems):
    copies = [pltpu.make_async_copy(s, t, sems.at[k]) for k, (s, t) in enumerate(zip(sources, targets))]
    for copy in copies:
        copy.start()
    for copy in copies:
        copy.wait()


def bond_masks(bonds, rows):
    last_x = lax.axis_index("gx") == lax.axis_size("gx") - 1
    last_y = lax.axis_index("gy") == lax.axis_size("gy") - 1
    down, side = (bonds[m, rows].astype(f32) for m in range(2))
    row = lax.broadcasted_iota(jnp.int32, down.shape, 0) + rows.start
    down = jnp.where(jnp.logical_and(last_x, row == ROWS - 1), 0.0, down)
    side = jnp.where(jnp.logical_and(last_y, lanes() == COLS - 1), 0.0, side)
    return down, side


def pack_rows(state_at, potential_at, bonds_at, to_prev, to_next, state, potential, bonds, sems):
    fetched((state_at, potential_at, bonds_at), (state, potential, bonds), sems)
    for ref, rows, skip in ((to_prev, slice(0, 16), 0), (to_next, slice(16, 32), 16 - DEPTH)):
        for f in range(FIELDS):
            part = state[f, rows].astype(f32)[skip : skip + DEPTH]
            ref[pl.ds(f, 8, stride=FIELDS), :] = part[:8]
            ref[8 * FIELDS + f : 8 * FIELDS + f + 1] = part[8:]
        down, side = bond_masks(bonds, rows)
        for m, value in enumerate((potential[rows], down, side)):
            ref[EDGE + 16 * m : EDGE + 16 * m + 16] = value


def turn_bulk(state_at, potential_at, bonds_at, wave, masks, heads, tails, state, potential, bonds, sems):
    fetched((state_at, potential_at, bonds_at), (state, potential, bonds), sems)
    for f in range(FIELDS):
        wave[pl.ds(f, ROWS, stride=FIELDS), :] = state[f].astype(f32)
    down, side = bond_masks(bonds, slice(0, ROWS))
    for m, value in enumerate((potential[...], down, side)):
        masks[m] = value
    for i in range(ROWS):
        rows = slice(THIN * i, THIN * i + THIN)
        heads[rows], tails[rows] = ends_of(wave, FIELDS * i)


def tall_mask(masks, above, below, m):
    at = EDGE + 16 * m
    pad = jnp.zeros((TALL_PAD - TALL, COLS), f32)
    return jnp.concatenate([above[at + 16 - DEPTH : at + 16], masks[m], below[at : at + DEPTH], pad], axis=0)


def row_ends(above, below, heads, tails):
    both = []
    for i in range(TALL):
        if DEPTH <= i < DEPTH + ROWS:
            rows = slice(THIN * (i - DEPTH), THIN * (i - DEPTH) + THIN)
            both.append((heads[rows], tails[rows]))
        else:
            ref, at = (above, i) if i < DEPTH else (below, i - DEPTH - ROWS)
            both.append(ends_of(ref, FIELDS * at))
    return both


def pack_columns(above, below, masks, heads, tails, on_chip, off_chip, own, own_masks):
    even = lax.axis_index("gy") % 2 == 0

    def send(rows, heads, tails):
        head, tail = packed(heads, 0), packed(tails, HALF - DEPTH)
        on_chip[rows] = jnp.where(even, tail, head)
        off_chip[rows] = jnp.where(even, head, tail)

    both = row_ends(above, below, heads, tails)
    for t in range(PLACES):
        parts = both[t::PLACES]
        send(slice(THIN * t, THIN * t + THIN), [p[0] for p in parts], [p[1] for p in parts])
    parts = []
    for m in range(3):
        mask = tall_mask(masks, above, below, m)
        parts.append(ends(mask, mask))
        own_masks[m] = own_strip(*parts[m])
    send(slice(THIN * PLACES, COL_MSG), [p[0] for p in parts], [p[1] for p in parts])
    for i in range(TALL):
        own[THIN * i : THIN * i + THIN] = own_strip(*both[i])


def spread_rows(spread, m, value, count=TALL):
    for i in range(count):
        spread[m, 8 * i : 8 * i + 8] = jnp.broadcast_to(value[i : i + 1], (8, COLS))


def hamilton(source, masks, wide, first, after, finish):
    many = BATCH if wide == THIN else 1

    def rows_of(i, some):
        return source[wide * i : wide * (i + some)].reshape(some, wide, COLS)

    def mask_of(m, i, some):
        one = masks[m, 8 * i : 8 * (i + some)].reshape(some, 8, COLS)
        return jnp.concatenate([one] * (wide // 8), axis=1)

    for i in range(first, after, many):
        some = min(many, after - i)
        here = rows_of(i, some)
        pot, down, side = (mask_of(m, i, some) for m in range(3))
        right = turn(here, -1)
        left = turn(side * here, 1)
        handed = mask_of(1, i - 1, some) * rows_of(i - 1, some)
        hop = (down * rows_of(i + 1, some) + handed) + (side * right + left)
        finish(slice(wide * i, wide * (i + some)), pot * here - hop)


def factors(coeffs):
    c0, c1, c2, c3 = (coeffs[k] for k in range(4))
    one = jnp.ones((1, COLS), f32)
    e3 = 4.0 * c3 / 125.0
    per = 1.0 / (one * e3)
    return one * (c0 + c2) * per, one * ((c1 + 3.0 * c3) / 5.0) * per, one * (2.0 * c2 / 25.0) * per, e3


def step_of(start, out, one, two, masks, wide, d, weights):
    a0, a1, a2, _ = weights

    half = wide // 2

    def put(ref, rows, value):
        ref[rows] = value.reshape(-1, COLS)

    def get(ref, rows):
        return ref[rows].reshape(-1, wide, COLS)

    def first(rows, value):
        put(one, rows, value)

    def second(rows, value):
        x = get(start, rows)
        put(two, rows, a1 * x - value)
        put(out, rows, a0 * x - a2 * value)

    def third(rows, value):
        kept = get(out, rows)
        parts = [kept[:, :half] + value[:, half:], kept[:, half:] - value[:, :half]]
        put(out, rows, jnp.concatenate(parts, axis=1))

    hamilton(start, masks, wide, d + 1, TALL - d - 1, first)
    hamilton(one, masks, wide, d + 2, TALL - d - 2, second)
    hamilton(two, masks, wide, d + 3, TALL - d - 3, third)


def evolve_main(coeffs, wave, above, below, masks, main, spread, cur, one, two):
    for m in range(3):
        spread_rows(spread, m, tall_mask(masks, above, below, m))
    cur[:EDGE] = above[:EDGE]
    cur[EDGE : EDGE + ROWS * FIELDS] = wave[...]
    cur[EDGE + ROWS * FIELDS :] = below[:EDGE]
    weights = factors(coeffs)
    for step in range(STEPS):
        step_of(cur, cur, one, two, spread, FIELDS, 3 * step, weights)
    main[...] = cur[EDGE : EDGE + ROWS * FIELDS]


def evolve_rest(
    coeffs, boundary, phase, main, own, own_masks, on_chip, off_chip, evolved, part, strip, one, two, spread, cells, flat
):
    even = lax.axis_index("gy") % 2 == 0

    def received(rows):
        a, b = on_chip[rows], off_chip[rows]
        return jnp.where(even, b, a), jnp.where(even, a, b)

    left, right = received(slice(THIN * PLACES, COL_MSG))
    for m in range(3):
        spread_rows(spread, m, join(left, own_masks[m], right, m))
    for t in range(PLACES):
        left, right = received(slice(THIN * t, THIN * t + THIN))
        for u in range(PIECES):
            i = t + u * PLACES
            if i < TALL:
                rows = slice(THIN * i, THIN * i + THIN)
                strip[rows] = join(left, own[rows], right, u)

    weights = factors(coeffs)
    for step in range(STEPS):
        step_of(strip, strip, one, two, spread, THIN, 3 * step, weights)

    e3 = weights[3]
    scale = e3 * e3 * e3
    for r in range(0, ROWS, CHUNK):
        rim = strip[THIN * (r + DEPTH) : THIN * (r + DEPTH + CHUNK)].reshape(CHUNK, THIN, COLS)
        rows = slice(FIELDS * r, FIELDS * (r + CHUNK))
        middle = main[rows].reshape(CHUNK, FIELDS, COLS)
        parts = []
        for g in range(GROUPS):
            mine, by = rim[:, 8 * (g // 2) : 8 * (g // 2) + 8], HALF * (g % 2)
            value = jnp.where(lanes() < DEPTH, turn(mine, -by - DEPTH), middle[:, 8 * g : 8 * g + 8])
            parts.append(jnp.where(lanes() >= COLS - DEPTH, turn(mine, HALF + DEPTH - by), value))
        done = jnp.concatenate(parts, axis=1) * scale
        cells[rows] = done.reshape(CHUNK * FIELDS, COLS)
        for k in range(CHUNK):
            flat[:, COLS * (r + k) : COLS * (r + k + 1)] = done[k].astype(jnp.bfloat16)
    for f in range(FIELDS):
        evolved[f] = cells[pl.ds(f, ROWS, stride=FIELDS), :].astype(jnp.bfloat16)

    first_col = lax.axis_index("gy") * COLS
    inside = (lanes() + first_col >= boundary[0]).astype(f32).astype(jnp.bfloat16)
    amps = flat[...]
    amps_right = jnp.concatenate([amps[:, COLS * r : COLS * r + COLS] * inside for r in range(ROWS)], axis=1)
    contract = (((1,), (1,)), ((), ()))
    total = lax.dot_general(amps, amps, contract, preferred_element_type=f32)
    right = lax.dot_general(amps, amps_right, contract, preferred_element_type=f32)
    n = FIELDS // 2
    total_re = total[:n, :n] + total[n:, n:]
    total_im = total[:n, n:] - total[n:, :n]
    right_re = right[:n, :n] + right[n:, n:]
    right_im = right[:n, n:] - right[n:, :n]
    cosine, sine, count = phase[0], phase[1], phase[2]
    over_re = (total_re + cosine * right_re - sine * right_im) * count
    over_im = (total_im + cosine * right_im + sine * right_re) * count
    wide = jnp.concatenate([over_re, over_im], axis=0)
    tiles = [wide[8 * g : 8 * g + 8] for g in range(GROUPS)] + [jnp.zeros((8, COLS - GROUPS * n), f32)]
    tile = jnp.concatenate(tiles, axis=1)
    for p in range(part.shape[0]):
        part[p] = tile


def call(kernel, outs, inputs, scalars=0, fetch=False, scratch=(), limit=8, flops=100_000):
    moved = sum(4 * x.size for x in inputs)
    shapes = [pltpu.VMEM(s, d) for s, d in scratch]
    if fetch:
        shapes += [pltpu.VMEM(x.shape, x.dtype) for x in inputs] + [pltpu.SemaphoreType.DMA((len(inputs),))]
    space = pltpu.HBM if fetch else pltpu.VMEM
    return pl.pallas_call(
        kernel,
        out_shape=[jax.ShapeDtypeStruct(s, d) for s, d in outs],
        in_specs=[pl.BlockSpec(memory_space=pltpu.SMEM if k < scalars else space) for k in range(len(inputs))],
        out_specs=[pl.BlockSpec(memory_space=pltpu.VMEM)] * len(outs),
        scratch_shapes=shapes,
        compiler_params=pltpu.CompilerParams(vmem_limit_bytes=limit * MIB),
        cost_estimate=pl.CostEstimate(flops=flops, bytes_accessed=moved, transcendentals=0),
    )(*inputs)


def added(parts, axis):
    return jnp.sum(lax.all_to_all(parts, axis, 0, 0, tiled=True), axis=0)


def on_device(state, potential, bonds, coeffs, boundary, counting):
    norbit = state.shape[1]
    peers_x, peers_y = lax.axis_size("gx"), lax.axis_size("gy")
    count = float(ROWS * COLS * peers_x * peers_y)
    phase = jnp.stack([jnp.cos(counting[0]) - 1.0, jnp.sin(counting[0]), jnp.float32(1.0 / count)])
    fields = state.reshape(FIELDS, ROWS, COLS)

    to_prev, to_next = call(pack_rows, [((ROW_MSG, COLS), f32)] * 2, (fields, potential, bonds), fetch=True)
    above = lax.ppermute(to_next, "gx", [(i, (i + 1) % peers_x) for i in range(peers_x)])
    below = lax.ppermute(to_prev, "gx", [(i, (i - 1) % peers_x) for i in range(peers_x)])
    thin_own = ((THIN * ROWS, COLS), f32)
    wave, masks, heads, tails = call(
        turn_bulk,
        [((ROWS * FIELDS, COLS), f32), ((3, ROWS, COLS), f32), thin_own, thin_own],
        (fields, potential, bonds),
        fetch=True,
    )
    tall, thin, spread = ((FIELDS * TALL, COLS), f32), ((THIN * TALL, COLS), f32), ((3, 8 * TALL, COLS), f32)
    on_chip, off_chip, own, own_masks = call(
        pack_columns,
        [((COL_MSG, COLS), f32), ((COL_MSG, COLS), f32), thin, ((3, TALL_PAD, COLS), f32)],
        (above, below, masks, heads, tails),
    )
    on_chip = lax.ppermute(on_chip, "gy", [(i, i ^ 1) for i in range(peers_y)])
    off_chip = lax.ppermute(off_chip, "gy", [(i, (i + 2 * (i % 2) - 1) % peers_y) for i in range(peers_y)])
    (main,) = call(
        evolve_main,
        [((FIELDS * ROWS, COLS), f32)],
        (coeffs, wave, above, below, masks),
        scalars=1,
        scratch=[spread] + [tall] * 3,
        limit=12,
        flops=20_000_000,
    )
    evolved, part = call(
        evolve_rest,
        [((FIELDS, ROWS, COLS), jnp.bfloat16), ((peers_y, 8, COLS), f32)],
        (coeffs, boundary, phase, main, own, own_masks, on_chip, off_chip),
        scalars=3,
        scratch=[thin] * 3 + [spread, ((FIELDS * ROWS, COLS), f32), ((FIELDS, ROWS * COLS), jnp.bfloat16)],
        limit=12,
        flops=10_000_000,
    )
    total = added(part, "gy")
    total = added(jnp.broadcast_to(total[None], (peers_x,) + total.shape), "gx")
    over = total[:, : GROUPS * norbit].reshape(8, GROUPS, norbit).transpose(1, 0, 2).reshape(2, norbit, norbit)
    return evolved.reshape(state.shape), over


def solution(mesh):
    return jax.shard_map(
        on_device,
        mesh=mesh,
        in_specs=(P(None, None, "gx", "gy"), P("gx", "gy"), P(None, "gx", "gy"), P(), P(), P()),
        out_specs=(P(None, None, "gx", "gy"), P()),
        check_vma=False,
    )
```

time: 319 us -> 73.9 us (0.23)
  blocking collectives: 129 us -> 36.6 us
  starting transfers between devices: 111 us -> 20.4 us
  waiting for transfers between devices: 49 us -> 0.99 us
  other arithmetic: 19 us -> 0.13 us
  Pallas kernels: 0 us -> 9.35 us
    psum x1 -> x0, blocking collectives: 129 us -> none  [on_device(): summed = lax.psum(partial_sums, ('gx', 'gy'))]
    ppermute x36 -> x4, starting transfers between devices: 111 us -> 20.4 us  [the longest x1 9.5 us: on_device(): lax.ppermute(to_prev, 'gx', [(i, (i - 1) % peers_x) for i in range(peers_...]
    ppermute x36 -> x4, waiting for transfers between devices: 49 us -> 0.99 us  [the longest x1 0.86 us: on_device(): lax.ppermute(to_prev, 'gx', [(i, (i - 1) % peers_x) for i in range(peers_...]
    all_to_all x0 -> x2, blocking collectives: none -> 36.6 us  [added(): return jnp.sum(lax.all_to_all(parts, axis, 0, 0, tiled=True), axis=0)]
    pallas_call x0 -> x5, Pallas kernels: none -> 9.35 us  [call(): pl.pallas_call(kernel, out_shape=[jax.ShapeDtypeStruct(s, d) for s, d in...]
    sub x5 -> x0, other arithmetic: 7.15 us -> none  [the longest x2 5.49 us: on_device(): coeffs[0] * term_zero[0] + coeffs[1] * term_one[1] - coeffs[2] * term_two[0]]
    mul x17 -> x0, other arithmetic: 6.26 us -> none  [the longest x6 4.45 us: hamilton(): moved_col = mask_col * wave]
    another operation x12 -> x1, other arithmetic: 4.74 us -> 0.08 us  [on_device(): jnp.stack([jnp.cos(counting[0]) - 1.0, jnp.sin(counting[0]), jnp.float32(...]
  transfers between devices with their start and end apart: 36 -> 4, of which waited for: 13 -> 2; matrix products, arithmetic and copies ran while one was open for 1% -> 0% of each run, Pallas kernels for 0% -> 6%
where the time goes in v2:
time: 73.9 us; the launch traced here: 73.4 us
  blocking collectives  36.6 us (50%)
  starting transfers between devices  20.4 us (28%)
  Pallas kernels  9.35 us (13%)
  local copies, waits for them, and re-layouts  3.78 us (5%)
  between operations  2.17 us (3%)
  waiting for transfers between devices  0.99 us (1%)
    all_to_all x2, blocking collectives, added(): return jnp.sum(lax.all_to_all(parts, axis, 0, 0, tiled=True), axis=0)  36.6 us
    ppermute x1, starting transfers between devices, on_device(): lax.ppermute(to_prev, 'gx', [(i, (i - 1) % peers_x) for i in range(peers_...  9.5 us
    pallas_call x5, Pallas kernels, call(): pl.pallas_call(kernel, out_shape=[jax.ShapeDtypeStruct(s, d) for s, d in...  9.35 us
    ppermute x1, starting transfers between devices, on_device(): lax.ppermute(to_next, 'gx', [(i, (i + 1) % peers_x) for i in range(peers_...  4.38 us
    ppermute x1, starting transfers between devices, on_device(): on_chip = lax.ppermute(on_chip, 'gy', [(i, i ^ 1) for i in range(peers_y)])  3.45 us
    ppermute x1, starting transfers between devices, on_device(): lax.ppermute(off_chip, 'gy', [(i, (i + 2 * (i % 2) - 1) % peers_y) for i...  3.1 us
    unnamed x8, local copies, waits for them, and re-layouts  3.07 us
  transfers between devices with their start and end apart: 4, of which 2 were waited for; matrix products, arithmetic and copies ran while one was open for 0% of the time, Pallas kernels for 6%

profile of v2, /device:TPU:1, one launch (start us, length us, event | category | flops | bytes accessed | tf_op | source)
XLA Modules:
  0.0 73.4 jit_solution(10320947480469216613)
XLA Ops:
  0.6 0.0 copy-start
  0.6 0.9 %copy-done = bf16[2,16,32,128]{3,2,1,0:T(8,128)(2,1)S(1)} copy-done((bf16[2,16,32,128]{3,2,1,0:T(8,128)(2,1)S(1)}, bf16[2,16,32,128]{3,2,1,0:T(8,128)(2,1)}, u32[]{:S(2)}) %copy-start) | copy-done | bytes 262168
  1.6 0.0 copy-start.1
  1.6 0.8 %copy-done.1 = s32[2,32,128]{2,1,0:T(8,128)S(1)} copy-done((s32[2,32,128]{2,1,0:T(8,128)S(1)}, s32[2,32,128]{2,1,0:T(8,128)}, u32[]{:S(2)}) %copy-start.1) | copy-done | bytes 32792
  2.3 0.7 copy-done.2
  3.1 0.3 shard_map.78
  3.4 4.4 %collective-permute-start = (f32[336,128]{1,0:T(8,128)S(1)}, f32[336,128]{1,0:T(8,128)S(1)}, u32[]{:S(2)}, u32[]{:S(2)}) collective-permute-start(f32[336,128]{1,0:T(8,128)S(1)} %get-tuple-element.15), channel_id=1, source_target_pairs={{0,32},{32,64},{64,96},{96,128},{128,160},{160,192},{192,224},{224... | collective-permute-start | bytes 516104 | tf_op jit(solution)/shard_map/ppermute | solution.py:320
  7.7 9.5 %collective-permute-start.1 = (f32[336,128]{1,0:T(8,128)S(1)}, f32[336,128]{1,0:T(8,128)S(1)}, u32[]{:S(2)}, u32[]{:S(2)}) collective-permute-start(f32[336,128]{1,0:T(8,128)S(1)} %get-tuple-element.16), channel_id=1, source_target_pairs={{0,480},{32,0},{64,32},{96,64},{128,96},{160,128},{192,160},{224,1... | collective-permute-start | bytes 516104 | tf_op jit(solution)/shard_map/ppermute | solution.py:321
  17.3 0.6 shard_map.77
  19.3 0.1 collective-permute-done.above
  19.4 0.9 %collective-permute-done.1.below = f32[336,128]{1,0:T(8,128)S(1)} collective-permute-done((f32[336,128]{1,0:T(8,128)S(1)}, f32[336,128]{1,0:T(8,128)S(1)}, u32[]{:S(2)}, u32[]{:S(2)}) %collective-permute-start.1) | collective-permute-done | bytes 172064 | tf_op jit(solution)/shard_map/ppermute | solution.py:321
  20.3 0.9 %shard_map.80 = (f32[184,128]{1,0:T(8,128)S(1)}, f32[184,128]{1,0:T(8,128)S(1)}, f32[800,128]{1,0:T(8,128)S(1)}, f32[3,56,128]{2,1,0:T(8,128)S(1)}) custom-call(f32[336,128]{1,0:T(8,128)S(1)} %collective-permute-done.above, f32[336,128]{1,0:T(8,128)S(1)} %collective-permute-done.1.below, f32[3,32,128]{2,1,0:T(8,128)S(1)} %get-tuple-element.17.masks, ...), custom_call_target="tpu_custom_call" | custom-call | flops 100000 | bytes 917504 | tf_op jit(solution)/shard_map/pallas_call | solution.py:297
  21.1 3.5 %collective-permute-start.2 = (f32[184,128]{1,0:T(8,128)S(1)}, f32[184,128]{1,0:T(8,128)S(1)}, u32[]{:S(2)}, u32[]{:S(2)}) collective-permute-start(f32[184,128]{1,0:T(8,128)S(1)} %get-tuple-element.22), channel_id=1, source_target_pairs={{0,1},{1,0},{2,3},{3,2},{4,5},{5,4},{6,7},{7,6},{8,9},{9,8},{10,11... | collective-permute-start | bytes 282632 | tf_op jit(solution)/shard_map/ppermute | solution.py:335
  24.6 3.1 %collective-permute-start.3 = (f32[184,128]{1,0:T(8,128)S(1)}, f32[184,128]{1,0:T(8,128)S(1)}, u32[]{:S(2)}, u32[]{:S(2)}) collective-permute-start(f32[184,128]{1,0:T(8,128)S(1)} %get-tuple-element.23), channel_id=1, source_target_pairs={{0,31},{1,2},{2,1},{3,4},{4,3},{5,6},{6,5},{7,8},{8,7},{9,10},{10,... | collective-permute-start | bytes 282632 | tf_op jit(solution)/shard_map/ppermute | solution.py:336
  27.7 0.1 pad_maximum_fusion.phase
  27.8 0.7 copy-done.3
  28.4 3.8 %shard_map.79.main = f32[1024,128]{1,0:T(8,128)S(1)} custom-call(f32[4]{0:T(128)S(1)} %copy-done.3, f32[1024,128]{1,0:T(8,128)S(1)} %get-tuple-element.14.wave, f32[336,128]{1,0:T(8,128)S(1)} %collective-permute-done.above, f32[336,128]{1,0:T(8,128)S(1)} %collective-permute-done.1.below, f32[3,32,128]{2,1,0:T(8,128)S(1)} %get-tuple-element.17.masks), custom_call_target="tpu_custom_call" | custom-call | flops 20000000 | bytes 917520 | tf_op jit(solution)/shard_map/pallas_call | solution.py:297
  32.2 0.0 collective-permute-done.2.on_chip
  32.2 0.0 collective-permute-done.3.off_chip
  32.2 3.8 %shard_map.81 = (bf16[32,32,128]{2,1,0:T(8,128)(2,1)}, f32[32,8,128]{2,1,0:T(8,128)S(1)}) custom-call(f32[4]{0:T(128)S(1)} %copy-done.3, s32[1]{0:T(128)S(6)} %copy.10.boundary, f32[3]{0:T(128)S(1)} %pad_maximum_fusion.phase, f32[1024,128]{1,0:T(8,128)S(1)} %shard_map.79.main, f32[800,128]{1,0:T(8,128)S(1)} %get-tuple-element.20.own, ...), custom_call_target="tpu_custom_call" | custom-call | flops 10000000 | bytes 1208352 | tf_op jit(solution)/shard_map/pallas_call | solution.py:297
  36.1 15.8 %all_to_all.10 = f32[32,8,128]{2,1,0:T(8,128)S(1)} all-to-all(f32[32,8,128]{2,1,0:T(8,128)S(1)} %get-tuple-element.25), channel_id=1, replica_groups=mesh['gx'=16,'gy'=32] {'gy'}, dimensions={0} | all-to-all | bytes 262144 | tf_op jit(solution)/shard_map/all_to_all | solution.py:309
  51.9 20.8 %all_to_all.11 = f32[16,8,128]{2,1,0:T(8,128)S(1)} all-to-all(f32[16,8,128]{2,1,0:T(8,128)S(1)} %broadcast_in_dim.2), channel_id=1, replica_groups=mesh['gx'=16,'gy'=32] {'gx'}, dimensions={0} | all-to-all | bytes 131072 | tf_op jit(solution)/shard_map/all_to_all | solution.py:309
  72.7 0.1 reshape.25
  72.8 0.6 copy.9
  (5 shorter events, 0.1 us)
Async XLA Ops:
  0.6 1.0 %copy-start = (bf16[2,16,32,128]{3,2,1,0:T(8,128)(2,1)S(1)}, bf16[2,16,32,128]{3,2,1,0:T(8,128)(2,1)}, u32[]{:S(2)}) copy-start(bf16[2,16,32,128]{3,2,1,0:T(8,128)(2,1)} %param.6) | copy-start | bytes 786436
  1.6 0.8 %copy-start.1 = (s32[2,32,128]{2,1,0:T(8,128)S(1)}, s32[2,32,128]{2,1,0:T(8,128)}, u32[]{:S(2)}) copy-start(s32[2,32,128]{2,1,0:T(8,128)} %bonds_at.3) | copy-start | bytes 98308
  2.3 0.7 copy-start.2
  3.4 16.0 %collective-permute-start = (f32[336,128]{1,0:T(8,128)S(1)}, f32[336,128]{1,0:T(8,128)S(1)}, u32[]{:S(2)}, u32[]{:S(2)}) collective-permute-start(f32[336,128]{1,0:T(8,128)S(1)} %get-tuple-element.15), channel_id=1, source_target_pairs={{0,32},{32,64},{64,96},{96,128},{128,160},{160,192},{192,224},{224... | collective-permute-start | bytes 516104 | tf_op jit(solution)/shard_map/ppermute | solution.py:320
  7.7 12.5 %collective-permute-start.1 = (f32[336,128]{1,0:T(8,128)S(1)}, f32[336,128]{1,0:T(8,128)S(1)}, u32[]{:S(2)}, u32[]{:S(2)}) collective-permute-start(f32[336,128]{1,0:T(8,128)S(1)} %get-tuple-element.16), channel_id=1, source_target_pairs={{0,480},{32,0},{64,32},{96,64},{128,96},{160,128},{192,160},{224,1... | collective-permute-start | bytes 516104 | tf_op jit(solution)/shard_map/ppermute | solution.py:321
  21.1 11.1 %collective-permute-start.2 = (f32[184,128]{1,0:T(8,128)S(1)}, f32[184,128]{1,0:T(8,128)S(1)}, u32[]{:S(2)}, u32[]{:S(2)}) collective-permute-start(f32[184,128]{1,0:T(8,128)S(1)} %get-tuple-element.22), channel_id=1, source_target_pairs={{0,1},{1,0},{2,3},{3,2},{4,5},{5,4},{6,7},{7,6},{8,9},{9,8},{10,11... | collective-permute-start | bytes 282632 | tf_op jit(solution)/shard_map/ppermute | solution.py:335
  24.6 7.6 %collective-permute-start.3 = (f32[184,128]{1,0:T(8,128)S(1)}, f32[184,128]{1,0:T(8,128)S(1)}, u32[]{:S(2)}, u32[]{:S(2)}) collective-permute-start(f32[184,128]{1,0:T(8,128)S(1)} %get-tuple-element.23), channel_id=1, source_target_pairs={{0,31},{1,2},{2,1},{3,4},{4,3},{5,6},{6,5},{7,8},{8,7},{9,10},{10,... | collective-permute-start | bytes 282632 | tf_op jit(solution)/shard_map/ppermute | solution.py:336
  27.8 0.7 copy-start.3

commit v3 on v2

--- a/solution.py
+++ b/solution.py
@@ -11,16 +11,19 @@
 GROUPS = 4
 HALF = COLS // 2
 TALL = ROWS + 2 * DEPTH
-TALL_PAD = 56
+TALL_PAD = 64
+QUARTER = TALL_PAD // 4
 BATCH = 16
 CHUNK = 8
 PIECES = 7
-PLACES = 8
+OWN_PLACES, PLACES = 5, 8
 EDGE = DEPTH * FIELDS
 THIN = 16
 ROW_MSG = EDGE + 3 * 16
-COL_MSG = THIN * PLACES + TALL_PAD
+COL_MSG = THIN * PLACES + QUARTER
+MORE = 8
 MIB = 1024 * 1024
+FIRST_LIMIT = 62
 
 f32 = jnp.float32
 
@@ -65,6 +68,28 @@
     groups = [ref[at + 8 * g : at + 8 * g + 8] for g in range(GROUPS)]
     both = [ends(groups[2 * p], groups[2 * p + 1]) for p in range(2)]
     return tuple(jnp.concatenate([pair[k] for pair in both], axis=0) for k in range(2))
+
+
+def pack_places(both, first, heads, tails):
+    for t in range(0, len(both), PIECES):
+        rows = slice(THIN * (first + t // PIECES), THIN * (first + t // PIECES) + THIN)
+        heads[rows] = packed([b[0] for b in both[t : t + PIECES]], 0)
+        tails[rows] = packed([b[1] for b in both[t : t + PIECES]], HALF - DEPTH)
+
+
+def folded(packed_masks):
+    quarter = lax.shift_right_logical(lanes(), 5)
+    out = packed_masks[:QUARTER]
+    for b in range(1, 4):
+        part = packed_masks[QUARTER * b : QUARTER * b + QUARTER]
+        out = jnp.where(quarter == b, turn(part, COLS // 4 * (b % 2)), out)
+    return out
+
+
+def unfolded(quarters):
+    low = lanes() < HALF
+    parts = [jnp.where(low, turn(quarters, -32 * b), turn(quarters, HALF - 32 * b)) for b in range(4)]
+    return jnp.concatenate(parts, axis=0)
 
 
 def fetched(sources, targets, sems):
@@ -97,16 +122,30 @@
             ref[EDGE + 16 * m : EDGE + 16 * m + 16] = value
 
 
-def turn_bulk(state_at, potential_at, bonds_at, wave, masks, heads, tails, state, potential, bonds, sems):
+def turn_bulk(
+    coeffs, boundary, phase, state_at, potential_at, bonds_at, wave, masks, heads, tails, own, consts,
+    state, potential, bonds, sems,
+):
     fetched((state_at, potential_at, bonds_at), (state, potential, bonds), sems)
     for f in range(FIELDS):
         wave[pl.ds(f, ROWS, stride=FIELDS), :] = state[f].astype(f32)
     down, side = bond_masks(bonds, slice(0, ROWS))
     for m, value in enumerate((potential[...], down, side)):
         masks[m] = value
+    both = []
     for i in range(ROWS):
-        rows = slice(THIN * i, THIN * i + THIN)
-        heads[rows], tails[rows] = ends_of(wave, FIELDS * i)
+        both.append(ends_of(wave, FIELDS * i))
+        own[THIN * i : THIN * i + THIN] = own_strip(*both[i])
+    pack_places(both, 0, heads, tails)
+    first_col = lax.axis_index("gy") * COLS
+    consts[:3] = jnp.concatenate(factors(coeffs), axis=0)
+    e3 = 4.0 * coeffs[3] / 125.0
+    one = jnp.ones((1, COLS), f32)
+    consts[3:4] = one * (e3 * e3 * e3)
+    consts[4:5] = one * phase[0]
+    consts[5:6] = one * phase[1]
+    consts[6:7] = one * phase[2]
+    consts[7:8] = (lanes() + first_col >= boundary[0]).astype(f32)
 
 
 def tall_mask(masks, above, below, m):
@@ -115,38 +154,30 @@
     return jnp.concatenate([above[at + 16 - DEPTH : at + 16], masks[m], below[at : at + DEPTH], pad], axis=0)
 
 
-def row_ends(above, below, heads, tails):
-    both = []
-    for i in range(TALL):
-        if DEPTH <= i < DEPTH + ROWS:
-            rows = slice(THIN * (i - DEPTH), THIN * (i - DEPTH) + THIN)
-            both.append((heads[rows], tails[rows]))
-        else:
-            ref, at = (above, i) if i < DEPTH else (below, i - DEPTH - ROWS)
-            both.append(ends_of(ref, FIELDS * at))
-    return both
-
-
-def pack_columns(above, below, masks, heads, tails, on_chip, off_chip, own, own_masks):
+def pack_columns(above, below, masks, heads, tails, off_chip, on_chip, own, own_masks, more_heads, more_tails):
     even = lax.axis_index("gy") % 2 == 0
 
-    def send(rows, heads, tails):
-        head, tail = packed(heads, 0), packed(tails, HALF - DEPTH)
+    def send(rows, head, tail):
         on_chip[rows] = jnp.where(even, tail, head)
         off_chip[rows] = jnp.where(even, head, tail)
 
-    both = row_ends(above, below, heads, tails)
-    for t in range(PLACES):
-        parts = both[t::PLACES]
-        send(slice(THIN * t, THIN * t + THIN), [p[0] for p in parts], [p[1] for p in parts])
+    both = [ends_of(ref, FIELDS * i) for ref in (above, below) for i in range(DEPTH)]
+    for i in range(2 * DEPTH):
+        own[THIN * i : THIN * i + THIN] = own_strip(*both[i])
+    pack_places(both, 0, more_heads, more_tails)
+    send(slice(0, THIN * OWN_PLACES), heads[...], tails[...])
+    send(slice(THIN * OWN_PLACES, THIN * PLACES), more_heads[...], more_tails[...])
     parts = []
     for m in range(3):
         mask = tall_mask(masks, above, below, m)
         parts.append(ends(mask, mask))
         own_masks[m] = own_strip(*parts[m])
-    send(slice(THIN * PLACES, COL_MSG), [p[0] for p in parts], [p[1] for p in parts])
-    for i in range(TALL):
-        own[THIN * i : THIN * i + THIN] = own_strip(*both[i])
+    off_chip[COL_MSG:] = jnp.zeros((MORE, COLS), f32)
+    send(
+        slice(THIN * PLACES, COL_MSG),
+        folded(packed([p[0] for p in parts], 0)),
+        folded(packed([p[1] for p in parts], HALF - DEPTH)),
+    )
 
 
 def spread_rows(spread, m, value, count=TALL):
@@ -178,13 +209,12 @@
 def factors(coeffs):
     c0, c1, c2, c3 = (coeffs[k] for k in range(4))
     one = jnp.ones((1, COLS), f32)
-    e3 = 4.0 * c3 / 125.0
-    per = 1.0 / (one * e3)
-    return one * (c0 + c2) * per, one * ((c1 + 3.0 * c3) / 5.0) * per, one * (2.0 * c2 / 25.0) * per, e3
+    per = 1.0 / (one * (4.0 * c3 / 125.0))
+    return one * (c0 + c2) * per, one * ((c1 + 3.0 * c3) / 5.0) * per, one * (2.0 * c2 / 25.0) * per
 
 
 def step_of(start, out, one, two, masks, wide, d, weights):
-    a0, a1, a2, _ = weights
+    a0, a1, a2 = weights
 
     half = wide // 2
 
@@ -212,20 +242,21 @@
     hamilton(two, masks, wide, d + 3, TALL - d - 3, third)
 
 
-def evolve_main(coeffs, wave, above, below, masks, main, spread, cur, one, two):
+def evolve_main(consts, wave, above, below, masks, main, spread, cur, one, two):
     for m in range(3):
         spread_rows(spread, m, tall_mask(masks, above, below, m))
     cur[:EDGE] = above[:EDGE]
     cur[EDGE : EDGE + ROWS * FIELDS] = wave[...]
     cur[EDGE + ROWS * FIELDS :] = below[:EDGE]
-    weights = factors(coeffs)
+    weights = [consts[k : k + 1] for k in range(3)]
     for step in range(STEPS):
         step_of(cur, cur, one, two, spread, FIELDS, 3 * step, weights)
     main[...] = cur[EDGE : EDGE + ROWS * FIELDS]
 
 
 def evolve_rest(
-    coeffs, boundary, phase, main, own, own_masks, on_chip, off_chip, evolved, part, strip, one, two, spread, cells, flat
+    consts, main, own, more_own, own_masks, on_chip, off_chip, evolved, part,
+    strip, one, two, spread, cells, flat, fields, sem,
 ):
     even = lax.axis_index("gy") % 2 == 0
 
@@ -233,23 +264,25 @@
         a, b = on_chip[rows], off_chip[rows]
         return jnp.where(even, b, a), jnp.where(even, a, b)
 
-    left, right = received(slice(THIN * PLACES, COL_MSG))
+    left, right = (unfolded(side) for side in received(slice(THIN * PLACES, COL_MSG)))
     for m in range(3):
         spread_rows(spread, m, join(left, own_masks[m], right, m))
     for t in range(PLACES):
         left, right = received(slice(THIN * t, THIN * t + THIN))
         for u in range(PIECES):
-            i = t + u * PLACES
-            if i < TALL:
-                rows = slice(THIN * i, THIN * i + THIN)
-                strip[rows] = join(left, own[rows], right, u)
-
-    weights = factors(coeffs)
+            i = PIECES * t + u
+            ref = own if t < OWN_PLACES else more_own
+            i = i if t < OWN_PLACES else i - PIECES * OWN_PLACES
+            if THIN * i < ref.shape[0]:
+                at = i + DEPTH if t < OWN_PLACES else (i if i < DEPTH else i + ROWS)
+                value = join(left, ref[THIN * i : THIN * i + THIN], right, u)
+                strip[THIN * at : THIN * at + THIN] = value
+
+    weights = [consts[k : k + 1] for k in range(3)]
     for step in range(STEPS):
         step_of(strip, strip, one, two, spread, THIN, 3 * step, weights)
 
-    e3 = weights[3]
-    scale = e3 * e3 * e3
+    scale = consts[3:4]
     for r in range(0, ROWS, CHUNK):
         rim = strip[THIN * (r + DEPTH) : THIN * (r + DEPTH + CHUNK)].reshape(CHUNK, THIN, COLS)
         rows = slice(FIELDS * r, FIELDS * (r + CHUNK))
@@ -261,13 +294,14 @@
             parts.append(jnp.where(lanes() >= COLS - DEPTH, turn(mine, HALF + DEPTH - by), value))
         done = jnp.concatenate(parts, axis=1) * scale
         cells[rows] = done.reshape(CHUNK * FIELDS, COLS)
-        for k in range(CHUNK):
-            flat[:, COLS * (r + k) : COLS * (r + k + 1)] = done[k].astype(jnp.bfloat16)
     for f in range(FIELDS):
-        evolved[f] = cells[pl.ds(f, ROWS, stride=FIELDS), :].astype(jnp.bfloat16)
-
-    first_col = lax.axis_index("gy") * COLS
-    inside = (lanes() + first_col >= boundary[0]).astype(f32).astype(jnp.bfloat16)
+        fields[f] = cells[pl.ds(f, ROWS, stride=FIELDS), :].astype(jnp.bfloat16)
+    leaving = pltpu.make_async_copy(fields, evolved, sem)
+    leaving.start()
+    for r in range(ROWS):
+        flat[:, COLS * r : COLS * (r + 1)] = cells[FIELDS * r : FIELDS * (r + 1)].astype(jnp.bfloat16)
+
+    inside = consts[7:8].astype(jnp.bfloat16)
     amps = flat[...]
     amps_right = jnp.concatenate([amps[:, COLS * r : COLS * r + COLS] * inside for r in range(ROWS)], axis=1)
     contract = (((1,), (1,)), ((), ()))
@@ -278,7 +312,7 @@
     total_im = total[:n, n:] - total[n:, :n]
     right_re = right[:n, :n] + right[n:, n:]
     right_im = right[:n, n:] - right[n:, :n]
-    cosine, sine, count = phase[0], phase[1], phase[2]
+    cosine, sine, count = (consts[k : k + 1, :n] for k in (4, 5, 6))
     over_re = (total_re + cosine * right_re - sine * right_im) * count
     over_im = (total_im + cosine * right_im + sine * right_re) * count
     wide = jnp.concatenate([over_re, over_im], axis=0)
@@ -286,22 +320,26 @@
     tile = jnp.concatenate(tiles, axis=1)
     for p in range(part.shape[0]):
         part[p] = tile
-
-
-def call(kernel, outs, inputs, scalars=0, fetch=False, scratch=(), limit=8, flops=100_000):
-    moved = sum(4 * x.size for x in inputs)
+    leaving.wait()
+
+
+def call(kernel, outs, inputs, scalars=0, fetched=0, sent=0, scratch=(), limit=8, flops=100_000):
+    many = len(inputs)
     shapes = [pltpu.VMEM(s, d) for s, d in scratch]
-    if fetch:
-        shapes += [pltpu.VMEM(x.shape, x.dtype) for x in inputs] + [pltpu.SemaphoreType.DMA((len(inputs),))]
-    space = pltpu.HBM if fetch else pltpu.VMEM
+    shapes += [pltpu.VMEM(x.shape, x.dtype) for x in inputs[many - fetched :]]
+    if fetched:
+        shapes.append(pltpu.SemaphoreType.DMA((fetched,)))
+    if sent:
+        shapes.append(pltpu.SemaphoreType.DMA)
+    spaces = [pltpu.SMEM] * scalars + [pltpu.VMEM] * (many - scalars - fetched) + [pltpu.HBM] * fetched
     return pl.pallas_call(
         kernel,
         out_shape=[jax.ShapeDtypeStruct(s, d) for s, d in outs],
-        in_specs=[pl.BlockSpec(memory_space=pltpu.SMEM if k < scalars else space) for k in range(len(inputs))],
-        out_specs=[pl.BlockSpec(memory_space=pltpu.VMEM)] * len(outs),
+        in_specs=[pl.BlockSpec(memory_space=space) for space in spaces],
+        out_specs=[pl.BlockSpec(memory_space=pltpu.HBM if k < sent else pltpu.VMEM) for k in range(len(outs))],
         scratch_shapes=shapes,
         compiler_params=pltpu.CompilerParams(vmem_limit_bytes=limit * MIB),
-        cost_estimate=pl.CostEstimate(flops=flops, bytes_accessed=moved, transcendentals=0),
+        cost_estimate=pl.CostEstimate(flops=flops, bytes_accessed=sum(4 * x.size for x in inputs), transcendentals=0),
     )(*inputs)
 
 
@@ -316,39 +354,56 @@
     phase = jnp.stack([jnp.cos(counting[0]) - 1.0, jnp.sin(counting[0]), jnp.float32(1.0 / count)])
     fields = state.reshape(FIELDS, ROWS, COLS)
 
-    to_prev, to_next = call(pack_rows, [((ROW_MSG, COLS), f32)] * 2, (fields, potential, bonds), fetch=True)
+    inputs = (fields, potential, bonds)
+    to_prev, to_next = call(pack_rows, [((ROW_MSG, COLS), f32)] * 2, inputs, fetched=3, limit=FIRST_LIMIT)
     above = lax.ppermute(to_next, "gx", [(i, (i + 1) % peers_x) for i in range(peers_x)])
     below = lax.ppermute(to_prev, "gx", [(i, (i - 1) % peers_x) for i in range(peers_x)])
-    thin_own = ((THIN * ROWS, COLS), f32)
-    wave, masks, heads, tails = call(
+    own_msg, more_msg = ((THIN * OWN_PLACES, COLS), f32), ((THIN * (PLACES - OWN_PLACES), COLS), f32)
+    wave, masks, heads, tails, own, consts = call(
         turn_bulk,
-        [((ROWS * FIELDS, COLS), f32), ((3, ROWS, COLS), f32), thin_own, thin_own],
-        (fields, potential, bonds),
-        fetch=True,
+        [
+            ((ROWS * FIELDS, COLS), f32),
+            ((3, ROWS, COLS), f32),
+            own_msg,
+            own_msg,
+            ((THIN * ROWS, COLS), f32),
+            ((8, COLS), f32),
+        ],
+        (coeffs, boundary, phase) + inputs,
+        scalars=3,
+        fetched=3,
     )
     tall, thin, spread = ((FIELDS * TALL, COLS), f32), ((THIN * TALL, COLS), f32), ((3, 8 * TALL, COLS), f32)
-    on_chip, off_chip, own, own_masks = call(
+    off_chip, on_chip, more_own, own_masks = call(
         pack_columns,
-        [((COL_MSG, COLS), f32), ((COL_MSG, COLS), f32), thin, ((3, TALL_PAD, COLS), f32)],
+        [
+            ((COL_MSG + MORE, COLS), f32),
+            ((COL_MSG, COLS), f32),
+            ((THIN * 2 * DEPTH, COLS), f32),
+            ((3, TALL_PAD, COLS), f32),
+        ],
         (above, below, masks, heads, tails),
-    )
+        scratch=[more_msg] * 2,
+    )
+    pairs = [(i, i + 2 * (i % 2) - 1) for i in range(1, peers_y - 1)]
+    off_chip = lax.ppermute(off_chip, "gy", pairs)
     on_chip = lax.ppermute(on_chip, "gy", [(i, i ^ 1) for i in range(peers_y)])
-    off_chip = lax.ppermute(off_chip, "gy", [(i, (i + 2 * (i % 2) - 1) % peers_y) for i in range(peers_y)])
     (main,) = call(
         evolve_main,
         [((FIELDS * ROWS, COLS), f32)],
-        (coeffs, wave, above, below, masks),
-        scalars=1,
+        (consts, wave, above, below, masks),
         scratch=[spread] + [tall] * 3,
         limit=12,
         flops=20_000_000,
     )
+    block = ((FIELDS, ROWS, COLS), jnp.bfloat16)
     evolved, part = call(
         evolve_rest,
-        [((FIELDS, ROWS, COLS), jnp.bfloat16), ((peers_y, 8, COLS), f32)],
-        (coeffs, boundary, phase, main, own, own_masks, on_chip, off_chip),
-        scalars=3,
-        scratch=[thin] * 3 + [spread, ((FIELDS * ROWS, COLS), f32), ((FIELDS, ROWS * COLS), jnp.bfloat16)],
+        [block, ((peers_y, 8, COLS), f32)],
+        (consts, main, own, more_own, own_masks, on_chip, off_chip),
+        sent=1,
+        scratch=[thin] * 3
+        + [spread, ((FIELDS * ROWS, COLS), f32), ((FIELDS, ROWS * COLS), jnp.bfloat16), block],
         limit=12,
         flops=10_000_000,
     )

time: 73.9 us -> 70.4 us (0.953)
  local copies, waits for them, and re-layouts: 3.78 us -> 1.28 us
  Pallas kernels: 9.35 us -> 11.8 us
  blocking collectives: 36.6 us -> 34.8 us
  waiting for transfers between devices: 0.99 us -> 0.01 us
    unnamed x8, local copies, waits for them, and re-layouts: 3.07 us -> 0.58 us
    pallas_call x5, Pallas kernels: 9.35 us -> 11.8 us  [call(): pl.pallas_call(kernel, out_shape=[jax.ShapeDtypeStruct(s, d) for s, d in...]
    all_to_all x2, blocking collectives: 36.6 us -> 34.8 us  [added(): return jnp.sum(lax.all_to_all(parts, axis, 0, 0, tiled=True), axis=0)]
    ppermute x1, starting transfers between devices: 3.45 us -> 1.92 us  [on_device(): on_chip = lax.ppermute(on_chip, 'gy', [(i, i ^ 1) for i in range(peers_y)])]
    ppermute x1, starting transfers between devices: 3.1 us -> 4.05 us  [on_device(): off_chip = lax.ppermute(off_chip, 'gy', pairs)]
    ppermute x1, waiting for transfers between devices: 0.86 us -> 0.01 us  [on_device(): lax.ppermute(to_prev, 'gx', [(i, (i - 1) % peers_x) for i in range(peers_...]
  transfers between devices with their start and end apart: 4 -> 4, of which waited for: 2 -> 0; matrix products, arithmetic and copies ran while one was open for 0% -> 0% of each run, Pallas kernels for 6% -> 9%
where the time goes in v3:
time: 70.4 us; the launch traced here: 70.1 us
  blocking collectives  34.8 us (49%)
  starting transfers between devices  19.8 us (28%)
  Pallas kernels  11.8 us (17%)
  between operations  2.22 us (3%)
  local copies, waits for them, and re-layouts  1.28 us (2%)
    all_to_all x2, blocking collectives, added(): return jnp.sum(lax.all_to_all(parts, axis, 0, 0, tiled=True), axis=0)  34.8 us
    pallas_call x5, Pallas kernels, call(): pl.pallas_call(kernel, out_shape=[jax.ShapeDtypeStruct(s, d) for s, d in...  11.8 us
    ppermute x1, starting transfers between devices, on_device(): lax.ppermute(to_prev, 'gx', [(i, (i - 1) % peers_x) for i in range(peers_...  9.5 us
    ppermute x1, starting transfers between devices, on_device(): lax.ppermute(to_next, 'gx', [(i, (i + 1) % peers_x) for i in range(peers_...  4.37 us
    ppermute x1, starting transfers between devices, on_device(): off_chip = lax.ppermute(off_chip, 'gy', pairs)  4.05 us
    ppermute x1, starting transfers between devices, on_device(): on_chip = lax.ppermute(on_chip, 'gy', [(i, i ^ 1) for i in range(peers_y)])  1.92 us
  transfers between devices with their start and end apart: 4, of which 0 were waited for; matrix products, arithmetic and copies ran while one was open for 0% of the time, Pallas kernels for 9%

profile of v3, /device:TPU:1, one launch (start us, length us, event | category | flops | bytes accessed | tf_op | source)
XLA Modules:
  0.0 70.1 jit_solution(14339057936000952221)
XLA Ops:
  0.6 0.0 copy-start
  0.6 0.0 copy-start.1
  0.6 0.0 copy-start.2
  0.7 1.9 %shard_map.78 = (f32[336,128]{1,0:T(8,128)}, f32[336,128]{1,0:T(8,128)}) custom-call(bf16[32,32,128]{2,1,0:T(8,128)(2,1)} %bitcast.5, f32[32,128]{1,0:T(8,128)} %potential_at.3, s32[2,32,128]{2,1,0:T(8,128)} %bonds_at.3), custom_call_target="tpu_custom_call" | custom-call | flops 100000 | bytes 573440 | tf_op jit(solution)/shard_map/pallas_call | solution.py:335
  2.6 4.4 %collective-permute-start = (f32[336,128]{1,0:T(8,128)}, f32[336,128]{1,0:T(8,128)S(1)}, u32[]{:S(2)}, u32[]{:S(2)}) collective-permute-start(f32[336,128]{1,0:T(8,128)} %get-tuple-element.18), channel_id=1, source_target_pairs={{0,32},{32,64},{64,96},{96,128},{128,160},{160,192},{192,224},{224... | collective-permute-start | bytes 516104 | tf_op jit(solution)/shard_map/ppermute | solution.py:359
  6.9 9.5 %collective-permute-start.1 = (f32[336,128]{1,0:T(8,128)}, f32[336,128]{1,0:T(8,128)S(1)}, u32[]{:S(2)}, u32[]{:S(2)}) collective-permute-start(f32[336,128]{1,0:T(8,128)} %get-tuple-element.19), channel_id=1, source_target_pairs={{0,480},{32,0},{64,32},{96,64},{128,96},{160,128},{192,160},{224,1... | collective-permute-start | bytes 516104 | tf_op jit(solution)/shard_map/ppermute | solution.py:360
  17.9 0.0 copy-start.3
  17.9 0.1 pad_maximum_fusion.phase
  18.0 0.0 copy-done
  18.0 0.6 copy-done.3
  18.5 2.8 %shard_map.77 = (f32[1024,128]{1,0:T(8,128)S(1)}, f32[3,32,128]{2,1,0:T(8,128)S(1)}, f32[80,128]{1,0:T(8,128)S(1)}, f32[80,128]{1,0:T(8,128)S(1)}, f32[512,128]{1,0:T(8,128)S(1)}, /*index=5*/f32[8,128]{1,0:T(8,128)S(1)}) custom-call(f32[4]{0:T(128)S(1)} %copy-done.3, s32[1]{0:T(128)S(6)} %copy.10.boundary, f32[3]{0:T(128)S(1)} %pad_maximum_fusion.phase, ...), custom_call_target="tpu_custom_call" | custom-call | flops 100000 | bytes 573472 | tf_op jit(solution)/shard_map/pallas_call | solution.py:335
  21.3 0.0 collective-permute-done.above
  21.3 0.0 collective-permute-done.1.below
  21.3 0.6 shard_map.80
  21.9 4.0 %collective-permute-start.3 = (f32[152,128]{1,0:T(8,128)S(1)}, f32[152,128]{1,0:T(8,128)S(1)}, u32[]{:S(2)}, u32[]{:S(2)}) collective-permute-start(f32[152,128]{1,0:T(8,128)S(1)} %get-tuple-element.27), channel_id=1, source_target_pairs={{1,2},{2,1},{3,4},{4,3},{5,6},{6,5},{7,8},{8,7},{9,10},{10,9},{11,... | collective-permute-start | bytes 233480 | tf_op jit(solution)/shard_map/ppermute | solution.py:389
  25.9 1.9 %collective-permute-start.2 = (f32[144,128]{1,0:T(8,128)S(1)}, f32[144,128]{1,0:T(8,128)S(1)}, u32[]{:S(2)}, u32[]{:S(2)}) collective-permute-start(f32[144,128]{1,0:T(8,128)S(1)} %get-tuple-element.26), channel_id=1, source_target_pairs={{0,1},{1,0},{2,3},{3,2},{4,5},{5,4},{6,7},{7,6},{8,9},{9,8},{10,11... | collective-permute-start | bytes 221192 | tf_op jit(solution)/shard_map/ppermute | solution.py:390
  27.9 3.2 %shard_map.79.main = f32[1024,128]{1,0:T(8,128)S(1)} custom-call(f32[8,128]{1,0:T(8,128)S(1)} %get-tuple-element.16.consts, f32[1024,128]{1,0:T(8,128)S(1)} %get-tuple-element.17.wave, f32[336,128]{1,0:T(8,128)S(1)} %collective-permute-done.above, f32[336,128]{1,0:T(8,128)S(1)} %collective-permute-done.1.below, f32[3,32,128]{2,1,0:T(8,128)S(1)} %get-tuple-element.20.masks), custom_call_target="tpu_custom_call" | custom-call | flops 20000000 | bytes 921600 | tf_op jit(solution)/shard_map/pallas_call | solution.py:335
  31.1 0.0 collective-permute-done.2.on_chip
  31.1 0.0 collective-permute-done.3.off_chip
  31.1 3.3 %shard_map.81 = (bf16[32,32,128]{2,1,0:T(8,128)(2,1)}, f32[32,8,128]{2,1,0:T(8,128)S(1)}) custom-call(f32[8,128]{1,0:T(8,128)S(1)} %get-tuple-element.16.consts, f32[1024,128]{1,0:T(8,128)S(1)} %shard_map.79.main, f32[512,128]{1,0:T(8,128)S(1)} %get-tuple-element.21.own, f32[288,128]{1,0:T(8,128)S(1)} %get-tuple-element.24.more_own, ...), custom_call_target="tpu_custom_call" | custom-call | flops 10000000 | bytes 1187840 | tf_op jit(solution)/shard_map/pallas_call | solution.py:335
  34.5 14.8 %all_to_all.10 = f32[32,8,128]{2,1,0:T(8,128)S(1)} all-to-all(f32[32,8,128]{2,1,0:T(8,128)S(1)} %get-tuple-element.29), channel_id=1, replica_groups=mesh['gx'=16,'gy'=32] {'gy'}, dimensions={0} | all-to-all | bytes 262144 | tf_op jit(solution)/shard_map/all_to_all | solution.py:347
  49.3 20.0 %all_to_all.11 = f32[16,8,128]{2,1,0:T(8,128)S(1)} all-to-all(f32[16,8,128]{2,1,0:T(8,128)S(1)} %broadcast_in_dim.2), channel_id=1, replica_groups=mesh['gx'=16,'gy'=32] {'gx'}, dimensions={0} | all-to-all | bytes 131072 | tf_op jit(solution)/shard_map/all_to_all | solution.py:347
  69.4 0.1 reshape.25
  69.5 0.6 copy.9
  (5 shorter events, 0.1 us)
Async XLA Ops:
  0.6 17.3 %copy-start = (bf16[2,16,32,128]{3,2,1,0:T(8,128)(2,1)S(1)}, bf16[2,16,32,128]{3,2,1,0:T(8,128)(2,1)}, u32[]{:S(2)}) copy-start(bf16[2,16,32,128]{3,2,1,0:T(8,128)(2,1)} %param.6) | copy-start | bytes 786436
  0.6 17.3 %copy-start.1 = (s32[2,32,128]{2,1,0:T(8,128)S(1)}, s32[2,32,128]{2,1,0:T(8,128)}, u32[]{:S(2)}) copy-start(s32[2,32,128]{2,1,0:T(8,128)} %bonds_at.3) | copy-start | bytes 98308
  0.6 17.3 %copy-start.2 = (f32[32,128]{1,0:T(8,128)S(1)}, f32[32,128]{1,0:T(8,128)}, u32[]{:S(2)}) copy-start(f32[32,128]{1,0:T(8,128)} %potential_at.3) | copy-start | bytes 49156
  2.6 18.8 %collective-permute-start = (f32[336,128]{1,0:T(8,128)}, f32[336,128]{1,0:T(8,128)S(1)}, u32[]{:S(2)}, u32[]{:S(2)}) collective-permute-start(f32[336,128]{1,0:T(8,128)} %get-tuple-element.18), channel_id=1, source_target_pairs={{0,32},{32,64},{64,96},{96,128},{128,160},{160,192},{192,224},{224... | collective-permute-start | bytes 516104 | tf_op jit(solution)/shard_map/ppermute | solution.py:359
  6.9 14.4 %collective-permute-start.1 = (f32[336,128]{1,0:T(8,128)}, f32[336,128]{1,0:T(8,128)S(1)}, u32[]{:S(2)}, u32[]{:S(2)}) collective-permute-start(f32[336,128]{1,0:T(8,128)} %get-tuple-element.19), channel_id=1, source_target_pairs={{0,480},{32,0},{64,32},{96,64},{128,96},{160,128},{192,160},{224,1... | collective-permute-start | bytes 516104 | tf_op jit(solution)/shard_map/ppermute | solution.py:360
  17.9 0.7 copy-start.3
  21.9 9.2 %collective-permute-start.3 = (f32[152,128]{1,0:T(8,128)S(1)}, f32[152,128]{1,0:T(8,128)S(1)}, u32[]{:S(2)}, u32[]{:S(2)}) collective-permute-start(f32[152,128]{1,0:T(8,128)S(1)} %get-tuple-element.27), channel_id=1, source_target_pairs={{1,2},{2,1},{3,4},{4,3},{5,6},{6,5},{7,8},{8,7},{9,10},{10,9},{11,... | collective-permute-start | bytes 233480 | tf_op jit(solution)/shard_map/ppermute | solution.py:389
  25.9 5.2 %collective-permute-start.2 = (f32[144,128]{1,0:T(8,128)S(1)}, f32[144,128]{1,0:T(8,128)S(1)}, u32[]{:S(2)}, u32[]{:S(2)}) collective-permute-start(f32[144,128]{1,0:T(8,128)S(1)} %get-tuple-element.26), channel_id=1, source_target_pairs={{0,1},{1,0},{2,3},{3,2},{4,5},{5,4},{6,7},{7,6},{8,9},{9,8},{10,11... | collective-permute-start | bytes 221192 | tf_op jit(solution)/shard_map/ppermute | solution.py:390

commit v4 on v3

--- a/solution.py
+++ b/solution.py
@@ -22,6 +22,7 @@
 ROW_MSG = EDGE + 3 * 16
 COL_MSG = THIN * PLACES + QUARTER
 MORE = 8
+PART = 4
 MIB = 1024 * 1024
 FIRST_LIMIT = 62
 
@@ -316,8 +317,9 @@
     over_re = (total_re + cosine * right_re - sine * right_im) * count
     over_im = (total_im + cosine * right_im + sine * right_re) * count
     wide = jnp.concatenate([over_re, over_im], axis=0)
-    tiles = [wide[8 * g : 8 * g + 8] for g in range(GROUPS)] + [jnp.zeros((8, COLS - GROUPS * n), f32)]
-    tile = jnp.concatenate(tiles, axis=1)
+    rows = [wide[8 * g : 8 * g + 8] for g in range(GROUPS)]
+    eight = jnp.concatenate(rows + rows, axis=1)
+    tile = jnp.where(lanes() < HALF, eight[:PART], eight[PART:])
     for p in range(part.shape[0]):
         part[p] = tile
     leaving.wait()
@@ -399,7 +401,7 @@
     block = ((FIELDS, ROWS, COLS), jnp.bfloat16)
     evolved, part = call(
         evolve_rest,
-        [block, ((peers_y, 8, COLS), f32)],
+        [block, ((peers_y, PART, COLS), f32)],
         (consts, main, own, more_own, own_masks, on_chip, off_chip),
         sent=1,
         scratch=[thin] * 3
@@ -409,7 +411,7 @@
     )
     total = added(part, "gy")
     total = added(jnp.broadcast_to(total[None], (peers_x,) + total.shape), "gx")
-    over = total[:, : GROUPS * norbit].reshape(8, GROUPS, norbit).transpose(1, 0, 2).reshape(2, norbit, norbit)
+    over = total.reshape(PART, 2, GROUPS, norbit).transpose(2, 1, 0, 3).reshape(2, norbit, norbit)
     return evolved.reshape(state.shape), over
 
 

time: 70.4 us -> 70 us (level)
  no operation moved by 1% of the time
where the time goes in v4:
time: 70 us; the launch traced here: 69.7 us
  blocking collectives  34.4 us (49%)
  starting transfers between devices  19.8 us (28%)
  Pallas kernels  11.8 us (17%)
  between operations  2.22 us (3%)
  local copies, waits for them, and re-layouts  1.29 us (2%)
    all_to_all x2, blocking collectives, added(): return jnp.sum(lax.all_to_all(parts, axis, 0, 0, tiled=True), axis=0)  34.4 us
    pallas_call x5, Pallas kernels, call(): pl.pallas_call(kernel, out_shape=[jax.ShapeDtypeStruct(s, d) for s, d in...  11.8 us
    ppermute x1, starting transfers between devices, on_device(): lax.ppermute(to_prev, 'gx', [(i, (i - 1) % peers_x) for i in range(peers_...  9.5 us
    ppermute x1, starting transfers between devices, on_device(): lax.ppermute(to_next, 'gx', [(i, (i + 1) % peers_x) for i in range(peers_...  4.37 us
    ppermute x1, starting transfers between devices, on_device(): off_chip = lax.ppermute(off_chip, 'gy', pairs)  4.05 us
    ppermute x1, starting transfers between devices, on_device(): on_chip = lax.ppermute(on_chip, 'gy', [(i, i ^ 1) for i in range(peers_y)])  1.92 us
  transfers between devices with their start and end apart: 4, of which 0 were waited for; matrix products, arithmetic and copies ran while one was open for 0% of the time, Pallas kernels for 9%

profile of v4, /device:TPU:1, one launch (start us, length us, event | category | flops | bytes accessed | tf_op | source)
XLA Modules:
  0.0 69.7 jit_solution(15385575781165238988)
XLA Ops:
  0.6 0.0 copy-start
  0.6 0.0 copy-start.1
  0.6 0.0 copy-start.2
  0.7 1.9 %shard_map.78 = (f32[336,128]{1,0:T(8,128)}, f32[336,128]{1,0:T(8,128)}) custom-call(bf16[32,32,128]{2,1,0:T(8,128)(2,1)} %bitcast.4, f32[32,128]{1,0:T(8,128)} %potential_at.3, s32[2,32,128]{2,1,0:T(8,128)} %bonds_at.3), custom_call_target="tpu_custom_call" | custom-call | flops 100000 | bytes 573440 | tf_op jit(solution)/shard_map/pallas_call | solution.py:337
  2.6 4.4 %collective-permute-start = (f32[336,128]{1,0:T(8,128)}, f32[336,128]{1,0:T(8,128)S(1)}, u32[]{:S(2)}, u32[]{:S(2)}) collective-permute-start(f32[336,128]{1,0:T(8,128)} %get-tuple-element.18), channel_id=1, source_target_pairs={{0,32},{32,64},{64,96},{96,128},{128,160},{160,192},{192,224},{224... | collective-permute-start | bytes 516104 | tf_op jit(solution)/shard_map/ppermute | solution.py:361
  6.9 9.5 %collective-permute-start.1 = (f32[336,128]{1,0:T(8,128)}, f32[336,128]{1,0:T(8,128)S(1)}, u32[]{:S(2)}, u32[]{:S(2)}) collective-permute-start(f32[336,128]{1,0:T(8,128)} %get-tuple-element.19), channel_id=1, source_target_pairs={{0,480},{32,0},{64,32},{96,64},{128,96},{160,128},{192,160},{224,1... | collective-permute-start | bytes 516104 | tf_op jit(solution)/shard_map/ppermute | solution.py:362
  17.9 0.0 copy-start.3
  17.9 0.1 pad_maximum_fusion.phase
  18.0 0.0 copy-done.1
  18.0 0.6 copy-done.3
  18.5 2.8 %shard_map.77 = (f32[1024,128]{1,0:T(8,128)S(1)}, f32[3,32,128]{2,1,0:T(8,128)S(1)}, f32[80,128]{1,0:T(8,128)S(1)}, f32[80,128]{1,0:T(8,128)S(1)}, f32[512,128]{1,0:T(8,128)S(1)}, /*index=5*/f32[8,128]{1,0:T(8,128)S(1)}) custom-call(f32[4]{0:T(128)S(1)} %copy-done.3, s32[1]{0:T(128)S(6)} %copy.13.boundary, f32[3]{0:T(128)S(1)} %pad_maximum_fusion.phase, ...), custom_call_target="tpu_custom_call" | custom-call | flops 100000 | bytes 573472 | tf_op jit(solution)/shard_map/pallas_call | solution.py:337
  21.3 0.0 collective-permute-done.above
  21.3 0.0 collective-permute-done.1.below
  21.3 0.6 shard_map.80
  21.9 4.0 %collective-permute-start.3 = (f32[152,128]{1,0:T(8,128)S(1)}, f32[152,128]{1,0:T(8,128)S(1)}, u32[]{:S(2)}, u32[]{:S(2)}) collective-permute-start(f32[152,128]{1,0:T(8,128)S(1)} %get-tuple-element.27), channel_id=1, source_target_pairs={{1,2},{2,1},{3,4},{4,3},{5,6},{6,5},{7,8},{8,7},{9,10},{10,9},{11,... | collective-permute-start | bytes 233480 | tf_op jit(solution)/shard_map/ppermute | solution.py:391
  25.9 1.9 %collective-permute-start.2 = (f32[144,128]{1,0:T(8,128)S(1)}, f32[144,128]{1,0:T(8,128)S(1)}, u32[]{:S(2)}, u32[]{:S(2)}) collective-permute-start(f32[144,128]{1,0:T(8,128)S(1)} %get-tuple-element.26), channel_id=1, source_target_pairs={{0,1},{1,0},{2,3},{3,2},{4,5},{5,4},{6,7},{7,6},{8,9},{9,8},{10,11... | collective-permute-start | bytes 221192 | tf_op jit(solution)/shard_map/ppermute | solution.py:392
  27.9 3.2 %shard_map.79.main = f32[1024,128]{1,0:T(8,128)S(1)} custom-call(f32[8,128]{1,0:T(8,128)S(1)} %get-tuple-element.16.consts, f32[1024,128]{1,0:T(8,128)S(1)} %get-tuple-element.17.wave, f32[336,128]{1,0:T(8,128)S(1)} %collective-permute-done.above, f32[336,128]{1,0:T(8,128)S(1)} %collective-permute-done.1.below, f32[3,32,128]{2,1,0:T(8,128)S(1)} %get-tuple-element.20.masks), custom_call_target="tpu_custom_call" | custom-call | flops 20000000 | bytes 921600 | tf_op jit(solution)/shard_map/pallas_call | solution.py:337
  31.1 0.0 collective-permute-done.2.on_chip
  31.1 0.0 collective-permute-done.3.off_chip
  31.1 3.3 %shard_map.81 = (bf16[32,32,128]{2,1,0:T(8,128)(2,1)}, f32[32,4,128]{2,1,0:T(4,128)S(1)}) custom-call(f32[8,128]{1,0:T(8,128)S(1)} %get-tuple-element.16.consts, f32[1024,128]{1,0:T(8,128)S(1)} %shard_map.79.main, f32[512,128]{1,0:T(8,128)S(1)} %get-tuple-element.21.own, f32[288,128]{1,0:T(8,128)S(1)} %get-tuple-element.24.more_own, ...), custom_call_target="tpu_custom_call" | custom-call | flops 10000000 | bytes 1187840 | tf_op jit(solution)/shard_map/pallas_call | solution.py:337
  34.5 14.5 %all_to_all.10 = f32[32,4,128]{2,1,0:T(4,128)S(1)} all-to-all(f32[32,4,128]{2,1,0:T(4,128)S(1)} %get-tuple-element.29), channel_id=1, replica_groups=mesh['gx'=16,'gy'=32] {'gy'}, dimensions={0} | all-to-all | bytes 131072 | tf_op jit(solution)/shard_map/all_to_all | solution.py:349
  49.0 19.9 %all_to_all.11 = f32[16,4,128]{2,1,0:T(4,128)S(1)} all-to-all(f32[16,4,128]{2,1,0:T(4,128)S(1)} %broadcast_in_dim.2), channel_id=1, replica_groups=mesh['gx'=16,'gy'=32] {'gx'}, dimensions={0} | all-to-all | bytes 65536 | tf_op jit(solution)/shard_map/all_to_all | solution.py:349
  68.9 0.1 reshape.25
  69.0 0.6 copy.11
  (5 shorter events, 0.1 us)
Async XLA Ops:
  0.6 17.3 %copy-start = (bf16[2,16,32,128]{3,2,1,0:T(8,128)(2,1)S(1)}, bf16[2,16,32,128]{3,2,1,0:T(8,128)(2,1)}, u32[]{:S(2)}) copy-start(bf16[2,16,32,128]{3,2,1,0:T(8,128)(2,1)} %param.6) | copy-start | bytes 786436
  0.6 17.3 %copy-start.1 = (s32[2,32,128]{2,1,0:T(8,128)S(1)}, s32[2,32,128]{2,1,0:T(8,128)}, u32[]{:S(2)}) copy-start(s32[2,32,128]{2,1,0:T(8,128)} %bonds_at.3) | copy-start | bytes 98308
  0.6 17.3 %copy-start.2 = (f32[32,128]{1,0:T(8,128)S(1)}, f32[32,128]{1,0:T(8,128)}, u32[]{:S(2)}) copy-start(f32[32,128]{1,0:T(8,128)} %potential_at.3) | copy-start | bytes 49156
  2.6 18.8 %collective-permute-start = (f32[336,128]{1,0:T(8,128)}, f32[336,128]{1,0:T(8,128)S(1)}, u32[]{:S(2)}, u32[]{:S(2)}) collective-permute-start(f32[336,128]{1,0:T(8,128)} %get-tuple-element.18), channel_id=1, source_target_pairs={{0,32},{32,64},{64,96},{96,128},{128,160},{160,192},{192,224},{224... | collective-permute-start | bytes 516104 | tf_op jit(solution)/shard_map/ppermute | solution.py:361
  6.9 14.4 %collective-permute-start.1 = (f32[336,128]{1,0:T(8,128)}, f32[336,128]{1,0:T(8,128)S(1)}, u32[]{:S(2)}, u32[]{:S(2)}) collective-permute-start(f32[336,128]{1,0:T(8,128)} %get-tuple-element.19), channel_id=1, source_target_pairs={{0,480},{32,0},{64,32},{96,64},{128,96},{160,128},{192,160},{224,1... | collective-permute-start | bytes 516104 | tf_op jit(solution)/shard_map/ppermute | solution.py:362
  17.9 0.7 copy-start.3
  21.9 9.2 %collective-permute-start.3 = (f32[152,128]{1,0:T(8,128)S(1)}, f32[152,128]{1,0:T(8,128)S(1)}, u32[]{:S(2)}, u32[]{:S(2)}) collective-permute-start(f32[152,128]{1,0:T(8,128)S(1)} %get-tuple-element.27), channel_id=1, source_target_pairs={{1,2},{2,1},{3,4},{4,3},{5,6},{6,5},{7,8},{8,7},{9,10},{10,9},{11,... | collective-permute-start | bytes 233480 | tf_op jit(solution)/shard_map/ppermute | solution.py:391
  25.9 5.2 %collective-permute-start.2 = (f32[144,128]{1,0:T(8,128)S(1)}, f32[144,128]{1,0:T(8,128)S(1)}, u32[]{:S(2)}, u32[]{:S(2)}) collective-permute-start(f32[144,128]{1,0:T(8,128)S(1)} %get-tuple-element.26), channel_id=1, source_target_pairs={{0,1},{1,0},{2,3},{3,2},{4,5},{5,4},{6,7},{7,6},{8,9},{9,8},{10,11... | collective-permute-start | bytes 221192 | tf_op jit(solution)/shard_map/ppermute | solution.py:392

commit v5 on v4

--- a/solution.py
+++ b/solution.py
@@ -19,7 +19,7 @@
 OWN_PLACES, PLACES = 5, 8
 EDGE = DEPTH * FIELDS
 THIN = 16
-ROW_MSG = EDGE + 3 * 16
+ROW_MSG = EDGE + 32
 COL_MSG = THIN * PLACES + QUARTER
 MORE = 8
 PART = 4
@@ -120,7 +120,8 @@
             ref[8 * FIELDS + f : 8 * FIELDS + f + 1] = part[8:]
         down, side = bond_masks(bonds, rows)
         for m, value in enumerate((potential[rows], down, side)):
-            ref[EDGE + 16 * m : EDGE + 16 * m + 16] = value
+            ref[EDGE + DEPTH * m : EDGE + DEPTH * m + DEPTH] = value[skip : skip + DEPTH]
+        ref[EDGE + 3 * DEPTH :] = jnp.zeros((ROW_MSG - EDGE - 3 * DEPTH, COLS), f32)
 
 
 def turn_bulk(
@@ -150,9 +151,9 @@
 
 
 def tall_mask(masks, above, below, m):
-    at = EDGE + 16 * m
+    at = EDGE + DEPTH * m
     pad = jnp.zeros((TALL_PAD - TALL, COLS), f32)
-    return jnp.concatenate([above[at + 16 - DEPTH : at + 16], masks[m], below[at : at + DEPTH], pad], axis=0)
+    return jnp.concatenate([above[at : at + DEPTH], masks[m], below[at : at + DEPTH], pad], axis=0)
 
 
 def pack_columns(above, below, masks, heads, tails, off_chip, on_chip, own, own_masks, more_heads, more_tails):

time: 70 us -> 70 us (level)
  no operation moved by 1% of the time
where the time goes in v5:
time: 70 us; the launch traced here: 69.7 us
  blocking collectives  34.4 us (49%)
  starting transfers between devices  19.8 us (28%)
  Pallas kernels  11.8 us (17%)
  between operations  2.22 us (3%)
  local copies, waits for them, and re-layouts  1.29 us (2%)
    all_to_all x2, blocking collectives, added(): return jnp.sum(lax.all_to_all(parts, axis, 0, 0, tiled=True), axis=0)  34.4 us
    pallas_call x5, Pallas kernels, call(): pl.pallas_call(kernel, out_shape=[jax.ShapeDtypeStruct(s, d) for s, d in...  11.8 us
    ppermute x1, starting transfers between devices, on_device(): lax.ppermute(to_prev, 'gx', [(i, (i - 1) % peers_x) for i in range(peers_...  9.5 us
    ppermute x1, starting transfers between devices, on_device(): lax.ppermute(to_next, 'gx', [(i, (i + 1) % peers_x) for i in range(peers_...  4.37 us
    ppermute x1, starting transfers between devices, on_device(): off_chip = lax.ppermute(off_chip, 'gy', pairs)  4.05 us
    ppermute x1, starting transfers between devices, on_device(): on_chip = lax.ppermute(on_chip, 'gy', [(i, i ^ 1) for i in range(peers_y)])  1.92 us
  transfers between devices with their start and end apart: 4, of which 0 were waited for; matrix products, arithmetic and copies ran while one was open for 0% of the time, Pallas kernels for 9%

profile of v5, /device:TPU:1, one launch (start us, length us, event | category | flops | bytes accessed | tf_op | source)
XLA Modules:
  0.0 69.7 jit_solution(580045661766774417)
XLA Ops:
  0.6 0.0 copy-start
  0.6 0.0 copy-start.1
  0.6 0.0 copy-start.2
  0.7 1.9 %shard_map.78 = (f32[320,128]{1,0:T(8,128)}, f32[320,128]{1,0:T(8,128)}) custom-call(bf16[32,32,128]{2,1,0:T(8,128)(2,1)} %bitcast.4, f32[32,128]{1,0:T(8,128)} %potential_at.3, s32[2,32,128]{2,1,0:T(8,128)} %bonds_at.3), custom_call_target="tpu_custom_call" | custom-call | flops 100000 | bytes 573440 | tf_op jit(solution)/shard_map/pallas_call | solution.py:338
  2.5 4.4 %collective-permute-start = (f32[320,128]{1,0:T(8,128)}, f32[320,128]{1,0:T(8,128)S(1)}, u32[]{:S(2)}, u32[]{:S(2)}) collective-permute-start(f32[320,128]{1,0:T(8,128)} %get-tuple-element.18), channel_id=1, source_target_pairs={{0,32},{32,64},{64,96},{96,128},{128,160},{160,192},{192,224},{224... | collective-permute-start | bytes 491528 | tf_op jit(solution)/shard_map/ppermute | solution.py:362
  6.9 9.5 %collective-permute-start.1 = (f32[320,128]{1,0:T(8,128)}, f32[320,128]{1,0:T(8,128)S(1)}, u32[]{:S(2)}, u32[]{:S(2)}) collective-permute-start(f32[320,128]{1,0:T(8,128)} %get-tuple-element.19), channel_id=1, source_target_pairs={{0,480},{32,0},{64,32},{96,64},{128,96},{160,128},{192,160},{224,1... | collective-permute-start | bytes 491528 | tf_op jit(solution)/shard_map/ppermute | solution.py:363
  17.9 0.0 copy-start.3
  17.9 0.1 pad_maximum_fusion.phase
  18.0 0.0 copy-done
  18.0 0.6 copy-done.3
  18.5 2.8 %shard_map.77 = (f32[1024,128]{1,0:T(8,128)S(1)}, f32[3,32,128]{2,1,0:T(8,128)S(1)}, f32[80,128]{1,0:T(8,128)S(1)}, f32[80,128]{1,0:T(8,128)S(1)}, f32[512,128]{1,0:T(8,128)S(1)}, /*index=5*/f32[8,128]{1,0:T(8,128)S(1)}) custom-call(f32[4]{0:T(128)S(1)} %copy-done.3, s32[1]{0:T(128)S(6)} %copy.13.boundary, f32[3]{0:T(128)S(1)} %pad_maximum_fusion.phase, ...), custom_call_target="tpu_custom_call" | custom-call | flops 100000 | bytes 573472 | tf_op jit(solution)/shard_map/pallas_call | solution.py:338
  21.3 0.0 collective-permute-done.above
  21.3 0.0 collective-permute-done.1.below
  21.3 0.6 shard_map.80
  21.9 4.0 %collective-permute-start.3 = (f32[152,128]{1,0:T(8,128)S(1)}, f32[152,128]{1,0:T(8,128)S(1)}, u32[]{:S(2)}, u32[]{:S(2)}) collective-permute-start(f32[152,128]{1,0:T(8,128)S(1)} %get-tuple-element.27), channel_id=1, source_target_pairs={{1,2},{2,1},{3,4},{4,3},{5,6},{6,5},{7,8},{8,7},{9,10},{10,9},{11,... | collective-permute-start | bytes 233480 | tf_op jit(solution)/shard_map/ppermute | solution.py:392
  25.9 1.9 %collective-permute-start.2 = (f32[144,128]{1,0:T(8,128)S(1)}, f32[144,128]{1,0:T(8,128)S(1)}, u32[]{:S(2)}, u32[]{:S(2)}) collective-permute-start(f32[144,128]{1,0:T(8,128)S(1)} %get-tuple-element.26), channel_id=1, source_target_pairs={{0,1},{1,0},{2,3},{3,2},{4,5},{5,4},{6,7},{7,6},{8,9},{9,8},{10,11... | collective-permute-start | bytes 221192 | tf_op jit(solution)/shard_map/ppermute | solution.py:393
  27.9 3.2 %shard_map.79.main = f32[1024,128]{1,0:T(8,128)S(1)} custom-call(f32[8,128]{1,0:T(8,128)S(1)} %get-tuple-element.16.consts, f32[1024,128]{1,0:T(8,128)S(1)} %get-tuple-element.17.wave, f32[320,128]{1,0:T(8,128)S(1)} %collective-permute-done.above, f32[320,128]{1,0:T(8,128)S(1)} %collective-permute-done.1.below, f32[3,32,128]{2,1,0:T(8,128)S(1)} %get-tuple-element.20.masks), custom_call_target="tpu_custom_call" | custom-call | flops 20000000 | bytes 905216 | tf_op jit(solution)/shard_map/pallas_call | solution.py:338
  31.1 0.0 collective-permute-done.2.on_chip
  31.1 0.0 collective-permute-done.3.off_chip
  31.1 3.4 %shard_map.81 = (bf16[32,32,128]{2,1,0:T(8,128)(2,1)}, f32[32,4,128]{2,1,0:T(4,128)S(1)}) custom-call(f32[8,128]{1,0:T(8,128)S(1)} %get-tuple-element.16.consts, f32[1024,128]{1,0:T(8,128)S(1)} %shard_map.79.main, f32[512,128]{1,0:T(8,128)S(1)} %get-tuple-element.21.own, f32[288,128]{1,0:T(8,128)S(1)} %get-tuple-element.24.more_own, ...), custom_call_target="tpu_custom_call" | custom-call | flops 10000000 | bytes 1187840 | tf_op jit(solution)/shard_map/pallas_call | solution.py:338
  34.5 14.5 %all_to_all.10 = f32[32,4,128]{2,1,0:T(4,128)S(1)} all-to-all(f32[32,4,128]{2,1,0:T(4,128)S(1)} %get-tuple-element.29), channel_id=1, replica_groups=mesh['gx'=16,'gy'=32] {'gy'}, dimensions={0} | all-to-all | bytes 131072 | tf_op jit(solution)/shard_map/all_to_all | solution.py:350
  49.0 19.9 %all_to_all.11 = f32[16,4,128]{2,1,0:T(4,128)S(1)} all-to-all(f32[16,4,128]{2,1,0:T(4,128)S(1)} %broadcast_in_dim.2), channel_id=1, replica_groups=mesh['gx'=16,'gy'=32] {'gx'}, dimensions={0} | all-to-all | bytes 65536 | tf_op jit(solution)/shard_map/all_to_all | solution.py:350
  69.0 0.1 reshape.25
  69.0 0.6 copy.11
  (5 shorter events, 0.1 us)
Async XLA Ops:
  0.6 17.3 %copy-start = (bf16[2,16,32,128]{3,2,1,0:T(8,128)(2,1)S(1)}, bf16[2,16,32,128]{3,2,1,0:T(8,128)(2,1)}, u32[]{:S(2)}) copy-start(bf16[2,16,32,128]{3,2,1,0:T(8,128)(2,1)} %param.6) | copy-start | bytes 786436
  0.6 17.3 %copy-start.1 = (s32[2,32,128]{2,1,0:T(8,128)S(1)}, s32[2,32,128]{2,1,0:T(8,128)}, u32[]{:S(2)}) copy-start(s32[2,32,128]{2,1,0:T(8,128)} %bonds_at.3) | copy-start | bytes 98308
  0.6 17.3 %copy-start.2 = (f32[32,128]{1,0:T(8,128)S(1)}, f32[32,128]{1,0:T(8,128)}, u32[]{:S(2)}) copy-start(f32[32,128]{1,0:T(8,128)} %potential_at.3) | copy-start | bytes 49156
  2.5 18.8 %collective-permute-start = (f32[320,128]{1,0:T(8,128)}, f32[320,128]{1,0:T(8,128)S(1)}, u32[]{:S(2)}, u32[]{:S(2)}) collective-permute-start(f32[320,128]{1,0:T(8,128)} %get-tuple-element.18), channel_id=1, source_target_pairs={{0,32},{32,64},{64,96},{96,128},{128,160},{160,192},{192,224},{224... | collective-permute-start | bytes 491528 | tf_op jit(solution)/shard_map/ppermute | solution.py:362
  6.9 14.4 %collective-permute-start.1 = (f32[320,128]{1,0:T(8,128)}, f32[320,128]{1,0:T(8,128)S(1)}, u32[]{:S(2)}, u32[]{:S(2)}) collective-permute-start(f32[320,128]{1,0:T(8,128)} %get-tuple-element.19), channel_id=1, source_target_pairs={{0,480},{32,0},{64,32},{96,64},{128,96},{160,128},{192,160},{224,1... | collective-permute-start | bytes 491528 | tf_op jit(solution)/shard_map/ppermute | solution.py:363
  17.9 0.7 copy-start.3
  21.9 9.3 %collective-permute-start.3 = (f32[152,128]{1,0:T(8,128)S(1)}, f32[152,128]{1,0:T(8,128)S(1)}, u32[]{:S(2)}, u32[]{:S(2)}) collective-permute-start(f32[152,128]{1,0:T(8,128)S(1)} %get-tuple-element.27), channel_id=1, source_target_pairs={{1,2},{2,1},{3,4},{4,3},{5,6},{6,5},{7,8},{8,7},{9,10},{10,9},{11,... | collective-permute-start | bytes 233480 | tf_op jit(solution)/shard_map/ppermute | solution.py:392
  25.9 5.2 %collective-permute-start.2 = (f32[144,128]{1,0:T(8,128)S(1)}, f32[144,128]{1,0:T(8,128)S(1)}, u32[]{:S(2)}, u32[]{:S(2)}) collective-permute-start(f32[144,128]{1,0:T(8,128)S(1)} %get-tuple-element.26), channel_id=1, source_target_pairs={{0,1},{1,0},{2,3},{3,2},{4,5},{5,4},{6,7},{7,6},{8,9},{9,8},{10,11... | collective-permute-start | bytes 221192 | tf_op jit(solution)/shard_map/ppermute | solution.py:393
